TPU v7x, 128 devices: a whole 4x4x4 slice. The times are simulated.
128 devices in a mesh: pulse: 8 (over y, core), tile: 16 (over z, x).
Axes of the slice: x: 4, y: 4, z: 4, core: 2. Of those that a mesh axis runs over, the one named last changes fastest.
Arguments:
- echoes: bfloat16 [65536, 2, 4096], P(('pulse', 'tile')), may hold values from -6 to 6
- phases: float32 [65536], P(('pulse', 'tile')), may hold values from -3.140625 to 3.140625
- kernel: bfloat16 [128, 256, 256], P(('pulse', 'tile')), may hold values from -0.375 to 0.375
- steering: bfloat16 [128, 12, 256, 1024], P(('pulse', 'tile')), may hold values from -0.0546875 to 0.0546875
- footprint: int32 [128, 12], P(('pulse', 'tile')), may hold values from 0 to 31, as said below
- counts: int32 [128], P(('pulse', 'tile')), may hold values from 1 to 12, as said below
- range_start: int32 [128, 2], P(('pulse', 'tile')), may hold values from 0 to 3840
Outputs:
- scene_tiles: float32 [2, 16, 256, 512], P(None, 'tile', 'pulse')
- phase_grad: float32 [65536], P(('pulse', 'tile'))
Inputs may be any that keep to these rules, and one draw needn't show every extreme that they name: `footprint`: only the first counts[b] entries of block b's list are used. The used entries of one block name tiles of distinct columns (id modulo 16). Some tile column is named by the used entries of every block. Some block uses all 12 entries. `counts`: some block has exactly 12.
All inputs are finite; a program needn't handle non-finite values.
Results may differ from a plain program's by a relative error of at most 0.0071.
Values may be sent and summed in bfloat16 or wider, within the bound.
A program may use at most 128 MiB of HBM per device.

v0:
```python
import math

import jax
import jax.numpy as jnp
from jax import lax
from jax.sharding import PartitionSpec as P


def phased(steer_slot, cosine, sines, pulses):
    real_part = steer_slot[:, :pulses].astype(jnp.float32)
    imag_part = steer_slot[:, pulses:].astype(jnp.float32)
    turned_re = real_part * cosine[None, :] - imag_part * sines[None, :]
    turned_im = real_part * sines[None, :] + imag_part * cosine[None, :]
    return jnp.concatenate([turned_re, turned_im], axis=1).astype(jnp.bfloat16)


def magnitude(scene, breadth):
    power = scene[..., :breadth] ** 2 + scene[..., breadth:] ** 2
    return (scene * jnp.concatenate([power, power], axis=-1)).astype(jnp.bfloat16)


def on_device(echoes, phases, kernel, steering, footprint, counts, range_start):
    columns = lax.axis_size("tile")
    row_parts = lax.axis_size("pulse")
    pulses = echoes.shape[0]
    window_len = kernel.shape[1]
    breadth = kernel.shape[2]
    height = steering.shape[2]
    slots = steering.shape[1]
    tile_rows = range_start.shape[1]
    anchor = jnp.zeros((), jnp.int32)
    live_count = counts[0]
    foot_ids = footprint[0]
    starts = range_start[0]
    interp = kernel[0]
    steer_all = steering[0]
    cosine = jnp.cos(phases)
    sines = jnp.sin(phases)
    owner_of = foot_ids % columns
    row_of = foot_ids // columns
    in_use = jnp.arange(slots, dtype=jnp.int32) < live_count
    matched = (owner_of[None, :] == jnp.arange(columns, dtype=jnp.int32)[:, None]) & in_use[None, :]
    selector = jnp.sum(jnp.where(matched, row_of[None, :] + 1, 0), axis=1) - 1

    def forward(slot, state_pair):
        buffer, stored = state_pair
        tile_id = foot_ids[slot]
        tile_row = tile_id // columns
        column = tile_id % columns
        window = lax.dynamic_slice_in_dim(echoes, starts[tile_row], window_len, 2).reshape(
            2 * pulses, window_len
        )
        profile = (
            jnp.dot(window, interp, preferred_element_type=jnp.float32)
            .astype(jnp.bfloat16)
            .reshape(pulses, 2 * breadth)
        )
        stacked = jnp.concatenate(
            [profile, jnp.concatenate([-profile[:, breadth:], profile[:, :breadth]], axis=1)],
            axis=0,
        )
        steer_ph = phased(steer_all[slot], cosine, sines, pulses)
        partial_value = jnp.dot(steer_ph, stacked, preferred_element_type=jnp.float32)
        buffer = lax.dynamic_update_slice(buffer, partial_value[None], (column, anchor, anchor))
        stored = lax.dynamic_update_slice(stored, profile[None], (slot, anchor, anchor))
        return (buffer, stored)

    buffer, stored = lax.fori_loop(
        jnp.int32(0),
        live_count,
        forward,
        (
            jnp.zeros((columns, height, 2 * breadth), jnp.float32),
            jnp.zeros((slots, pulses, 2 * breadth), jnp.bfloat16),
        ),
    )
    part_rows = height // row_parts
    tile_index = jnp.arange(tile_rows, dtype=jnp.int32)[:, None]
    blocks = buffer.reshape(columns, row_parts, part_rows, 2 * breadth)
    labels = jnp.broadcast_to(selector[:, None], (columns, row_parts))
    arrived, arrived_rows = (
        lax.all_to_all(
            lax.all_to_all(blocks, "pulse", split_axis=1, concat_axis=1, tiled=True),
            "tile",
            split_axis=0,
            concat_axis=0,
            tiled=True,
        ),
        lax.all_to_all(
            lax.all_to_all(labels, "pulse", split_axis=1, concat_axis=1, tiled=True),
            "tile",
            split_axis=0,
            concat_axis=0,
            tiled=True,
        ),
    )
    picker = (arrived_rows.reshape(-1)[None, :] == tile_index).astype(jnp.float32)
    scene = jnp.dot(
        picker,
        arrived.reshape(columns * row_parts, -1),
        precision=lax.Precision.HIGHEST,
        preferred_element_type=jnp.float32,
    ).reshape(tile_rows, part_rows, 2 * breadth)
    weight = magnitude(scene, breadth)
    outgoing = jnp.dot(
        picker.T.astype(jnp.bfloat16),
        weight.reshape(tile_rows, -1),
        preferred_element_type=jnp.float32,
    ).astype(jnp.bfloat16)
    outgoing = outgoing.reshape(columns, row_parts, part_rows, 2 * breadth)
    returned = lax.all_to_all(
        lax.all_to_all(outgoing, "pulse", split_axis=1, concat_axis=1, tiled=True),
        "tile",
        split_axis=0,
        concat_axis=0,
        tiled=True,
    )
    returned = returned.reshape(columns, height, 2 * breadth)

    def backward(slot, gradient):
        tile_id = foot_ids[slot]
        column = tile_id % columns
        profile = stored[slot]
        steer_ph = phased(steer_all[slot], cosine, sines, pulses).astype(jnp.float32)
        weight_tile = lax.dynamic_index_in_dim(returned, column, 0, keepdims=False)
        paired = jnp.concatenate(
            [profile, jnp.concatenate([profile[:, breadth:], -profile[:, :breadth]], axis=1)],
            axis=0,
        )
        moments = lax.dot_general(
            weight_tile, paired, (((1,), (1,)), ((), ())), preferred_element_type=jnp.float32
        )
        term = (
            steer_ph[:, :pulses] * moments[:, pulses:] + steer_ph[:, pulses:] * moments[:, :pulses]
        )
        return gradient + jnp.sum(term, axis=0)

    gradient = lax.fori_loop(jnp.int32(0), live_count, backward, jnp.zeros((pulses,), jnp.float32))
    factor = -4.0 / math.sqrt(height * breadth)
    return (scene[:, None], gradient * factor)


def solution(mesh):
    placed = (
        P(("pulse", "tile"), None, None),
        P(("pulse", "tile")),
        P(("pulse", "tile"), None, None),
        P(("pulse", "tile"), None, None, None),
        P(("pulse", "tile"), None),
        P(("pulse", "tile")),
        P(("pulse", "tile"), None),
    )
    return jax.shard_map(
        on_device,
        mesh=mesh,
        in_specs=placed,
        out_specs=(P(None, "tile", "pulse", None), P(("pulse", "tile"))),
        check_vma=False,
    )
```

profile of v0, /device:TPU:41, one launch (start us, length us, event | category | flops | bytes accessed | tf_op | source)
XLA Modules:
  0.0 645.5 jit_solution(11297405829009686326)
XLA Ops:
  2.7 5.2 all-to-all-start
  8.7 4.3 broadcast_in_dim.52
  13.0 3.2 broadcast_in_dim.53
  16.2 151.6 %while.26 = (s32[]{:T(128)}, f32[16,256,512]{2,1,0:T(8,128)}, bf16[12,512,512]{2,1,0:T(8,128)(2,1)}, s32[]{:T(128)}, bf16[12,256,1024]{2,1,0:T(8,128)(2,1)}, /*i...) while((s32[]{:T(128)}, f32[16,256,512]{2,1,0:T(8,128)}, ...), condition=%wide.region_2.3_spmd, body=%wide.region_1.2_spmd.sunk | while | flops 408551456 | bytes 11670048 | solution.py:68
  22.5 2.0 constant_dynamic-slice_fusion.2
  26.5 1.2 fusion.60
  35.1 2.0 constant_dynamic-slice_fusion.2
  39.1 1.2 fusion.60
  47.6 2.0 constant_dynamic-slice_fusion.2
  51.6 1.2 fusion.60
  60.2 2.0 constant_dynamic-slice_fusion.2
  64.2 1.2 fusion.60
  72.8 2.0 constant_dynamic-slice_fusion.2
  76.7 1.3 fusion.60
  85.4 2.0 constant_dynamic-slice_fusion.2
  89.3 1.2 fusion.60
  97.9 2.0 constant_dynamic-slice_fusion.2
  101.9 1.2 fusion.60
  110.5 2.0 constant_dynamic-slice_fusion.2
  114.5 1.2 fusion.60
  123.1 2.0 constant_dynamic-slice_fusion.2
  127.1 1.3 fusion.60
  135.7 2.0 constant_dynamic-slice_fusion.2
  139.7 1.2 fusion.60
  148.3 2.0 constant_dynamic-slice_fusion.2
  152.2 1.3 fusion.60
  160.9 2.0 constant_dynamic-slice_fusion.2
  164.9 1.3 fusion.60
  167.8 8.5 %copy.31 = f32[16,8,32,512]{3,2,0,1:T(8,128)} copy(f32[16,8,32,512]{3,2,1,0:T(8,128)} %bitcast.70) | data formatting | bytes 16777216 | tf_op jit(solution)/shard_map/reshape | solution.py:79
  176.3 4.9 all-to-all-start.2
  181.9 90.2 %all-to-all-done.2 = f32[16,8,32,512]{3,2,0,1:T(8,128)} async-done(((f32[16,8,32,512]{3,2,0,1:T(8,128)}), f32[16,8,32,512]{3,2,0,1:T(8,128)}, u32[]{:S(2)}, u32[]{:S(2)}) %all-to-all-start.2) | async-done | bytes 8388640 | tf_op jit(solution)/shard_map/all_to_all | solution.py:83
  272.1 3.4 all-to-all-start.1
  275.5 8.5 %copy.32 = f32[16,8,32,512]{3,2,1,0:T(8,128)} copy(f32[16,8,32,512]{3,2,0,1:T(8,128)} %all-to-all-done.2) | data formatting | bytes 16777216 | tf_op jit(solution)/shard_map/all_to_all | solution.py:83
  284.0 6.0 all-to-all-start.3
  291.3 119.3 %all-to-all-done.3 = f32[16,8,32,512]{3,2,1,0:T(8,128)} async-done(((f32[16,8,32,512]{3,2,1,0:T(8,128)}), f32[16,8,32,512]{3,2,1,0:T(8,128)}, u32[]{:S(2)}, u32[]{:S(2)}) %all-to-all-start.3) | async-done | bytes 8388640 | tf_op jit(solution)/shard_map/all_to_all | solution.py:82
  410.6 9.9 %copy.36 = f32[16,8,32,512]{3,1,2,0:T(8,128)S(1)} copy(f32[16,8,32,512]{3,2,1,0:T(8,128)} %all-to-all-done.3) | data formatting | bytes 16777216
  420.5 2.8 fusion.33
  423.5 1.3 convolution_convert_fusion.1
  424.8 1.4 copy.33
  426.2 57.3 %all_to_all.35 = bf16[16,8,32,512]{3,2,0,1:T(8,128)(2,1)S(1)} all-to-all(bf16[16,8,32,512]{3,2,0,1:T(8,128)(2,1)S(1)} %copy.33), channel_id=1, replica_groups=mesh['pulse'=8,'tile'=16] {'pulse'}, dimensions={1} | all-to-all | bytes 8388608 | tf_op jit(solution)/shard_map/all_to_all | solution.py:112
  483.6 2.5 copy.34
  486.0 6.5 %all-to-all-start.5 = ((bf16[16,8,32,512]{3,2,1,0:T(8,128)(2,1)}), bf16[16,8,32,512]{3,2,1,0:T(8,128)(2,1)}, u32[]{:S(2)}, u32[]{:S(2)}) async-start(bf16[16,8,32,512]{3,2,1,0:T(8,128)(2,1)} %copy.34), calls=%async_computation.5 | async-start | bytes 8388608 | tf_op jit(solution)/shard_map/all_to_all | solution.py:111
  492.6 60.8 %all-to-all-done.5 = bf16[16,8,32,512]{3,2,1,0:T(8,128)(2,1)} async-done(((bf16[16,8,32,512]{3,2,1,0:T(8,128)(2,1)}), bf16[16,8,32,512]{3,2,1,0:T(8,128)(2,1)}, u32[]{:S(2)}, u32[]{:S(2)}) %all-to-all-start.5) | async-done | bytes 4194336 | tf_op jit(solution)/shard_map/all_to_all | solution.py:111
  553.4 91.4 %while.27 = (s32[]{:T(128)}, f32[512]{0:T(512)S(1)}, s32[]{:T(128)}, bf16[12,256,1024]{2,1,0:T(8,128)(2,1)}, f32[512]{0:T(512)S(1)}, /*index=5*/f32[512]{0:T(512...) while((s32[]{:T(128)}, f32[512]{0:T(512)S(1)}, ...), condition=%wide.region_5.6_spmd, body=%wide.region_3.5_spmd.sunk | while | flops 274595872 | bytes 10236238 | solution.py:138
  556.8 1.1 dynamic-slice_bitcast_fusion.7
  557.9 1.4 fusion.64
  564.4 1.1 dynamic-slice_bitcast_fusion.7
  565.5 1.4 fusion.64
  571.9 1.1 dynamic-slice_bitcast_fusion.7
  573.1 1.4 fusion.64
  579.5 1.1 dynamic-slice_bitcast_fusion.7
  580.6 1.4 fusion.64
  587.1 1.1 dynamic-slice_bitcast_fusion.7
  588.2 1.4 fusion.64
  595.8 1.4 fusion.64
  603.3 1.4 fusion.64
  609.8 1.1 dynamic-slice_bitcast_fusion.7
  610.9 1.4 fusion.64
  617.3 1.1 dynamic-slice_bitcast_fusion.7
  618.5 1.4 fusion.64
  626.0 1.4 fusion.64
  633.6 1.4 fusion.64
  640.0 1.1 dynamic-slice_bitcast_fusion.7
  641.2 1.4 fusion.64
  (234 shorter events, 88.0 us)
Async XLA Ops:
  2.7 173.6 %all-to-all-start = ((s32[16,8,1]{0,2,1:T(1,128)}), s32[16,8,1]{0,2,1:T(1,128)S(1)}, u32[]{:S(2)}, u32[]{:S(2)}) async-start(s32[16,8,1]{0,2,1:T(1,128)} %broadcast_in_dim.51), calls=%async_computation | async-start | bytes 8192 | tf_op jit(solution)/shard_map/all_to_all | solution.py:90
  8.6 7.5 %copy-start = (bf16[1,256,256]{2,1,0:T(8,128)(2,1)S(1)}, bf16[1,256,256]{2,1,0:T(8,128)(2,1)}, u32[]{:S(2)}) copy-start(bf16[1,256,256]{2,1,0:T(8,128)(2,1)} %param.13) | copy-start | bytes 393220
  8.7 7.5 %copy-start.2 = (s32[1,2]{1,0:T(1,128)S(1)}, s32[1,2]{1,0:T(1,128)}, u32[]{:S(2)}) copy-start(s32[1,2]{1,0:T(1,128)} %param.17) | copy-start | bytes 28
  8.7 7.5 %copy-start.3 = (s32[1,12]{1,0:T(1,128)S(1)}, s32[1,12]{1,0:T(1,128)}, u32[]{:S(2)}) copy-start(s32[1,12]{1,0:T(1,128)} %param.15) | copy-start | bytes 148
  176.3 95.8 %all-to-all-start.2 = ((f32[16,8,32,512]{3,2,0,1:T(8,128)}), f32[16,8,32,512]{3,2,0,1:T(8,128)}, u32[]{:S(2)}, u32[]{:S(2)}) async-start(f32[16,8,32,512]{3,2,0,1:T(8,128)} %copy.31), calls=%async_computation.2 | async-start | bytes 16777216 | tf_op jit(solution)/shard_map/all_to_all | solution.py:83
  272.1 11.9 %all-to-all-start.1 = ((s32[16,1,8]{2,1,0:T(1,128)}), s32[16,1,8]{2,1,0:T(1,128)S(1)}, u32[]{:S(2)}, u32[]{:S(2)}) async-start(s32[16,1,8]{2,1,0:T(1,128)} %copy.30), calls=%async_computation.1 | async-start | bytes 16384 | tf_op jit(solution)/shard_map/all_to_all | solution.py:89
  284.0 126.7 %all-to-all-start.3 = ((f32[16,8,32,512]{3,2,1,0:T(8,128)}), f32[16,8,32,512]{3,2,1,0:T(8,128)}, u32[]{:S(2)}, u32[]{:S(2)}) async-start(f32[16,8,32,512]{3,2,1,0:T(8,128)} %copy.32), calls=%async_computation.3 | async-start | bytes 16777216 | tf_op jit(solution)/shard_map/all_to_all | solution.py:82
  423.4 2.9 copy-start.1
  486.0 67.4 %all-to-all-start.5 = ((bf16[16,8,32,512]{3,2,1,0:T(8,128)(2,1)}), bf16[16,8,32,512]{3,2,1,0:T(8,128)(2,1)}, u32[]{:S(2)}, u32[]{:S(2)}) async-start(bf16[16,8,32,512]{3,2,1,0:T(8,128)(2,1)} %copy.34), calls=%async_computation.5 | async-start | bytes 8388608 | tf_op jit(solution)/shard_map/all_to_all | solution.py:111
where the time goes:
time: 650 us; the launch traced here: 645 us
  waiting for transfers between devices  270 us (42%)
  local copies, waits for them, and re-layouts  144 us (22%)
  loops' own time  95.6 us (15%)
  blocking collectives  57.3 us (9%)
  matrix products  39.6 us (6%)
  starting transfers between devices  26.1 us (4%)
  other arithmetic  11.4 us (2%)
    all_to_all x1, waiting for transfers between devices, on_device(): lax.all_to_all(lax.all_to_all(blocks, 'pulse', split_axis=1, concat_axis=...  119 us
    all_to_all x1, waiting for transfers between devices, on_device(): lax.all_to_all(blocks, 'pulse', split_axis=1, concat_axis=1, tiled=True)  90.2 us
    another operation x1, loops' own time, on_device(): lax.fori_loop(jnp.int32(0), live_count, forward, (jnp.zeros((columns, hei...  61.8 us
    all_to_all x1, waiting for transfers between devices, on_device(): lax.all_to_all(lax.all_to_all(outgoing, 'pulse', split_axis=1, concat_axi...  60.8 us
    all_to_all x1, blocking collectives, on_device(): lax.all_to_all(outgoing, 'pulse', split_axis=1, concat_axis=1, tiled=True)  57.3 us
    another operation x1, loops' own time, on_device(): lax.fori_loop(jnp.int32(0), live_count, backward, jnp.zeros((pulses,), jn...  33.8 us
    dynamic_slice x12, local copies, waits for them, and re-layouts, forward(): lax.dynamic_slice_in_dim(echoes, starts[tile_row], window_len, 2)  23.6 us
    dot_general x12, matrix products, backward(): lax.dot_general(weight_tile, paired, (((1,), (1,)), ((), ())), preferred_...  17 us
  transfers between devices with their start and end apart: 5, of which 3 were waited for; matrix products, arithmetic and copies ran while one was open for 18% of the time, Pallas kernels for 0%

commit v1 on v0

v1 whole, which is shorter than its diff:
```python
import functools
import math

import jax
import jax.numpy as jnp
from jax import lax
from jax.experimental import pallas as pl
from jax.experimental.pallas import tpu as pltpu
from jax.sharding import PartitionSpec as P

MESH = pl.DeviceIdType.MESH
SIDE = 4
LANE = 128
SUB = 16
PARTS = (
    (0, 5, (0, 1, 2)),
    (5, 10, (1, 2, 0)),
    (10, 16, (2, 0, 1)),
)


def position():
    p = lax.axis_index("pulse")
    t = lax.axis_index("tile")
    return (p // 2, t // SIDE, t % SIDE), p % 2


def device_at(where, core):
    return (where[0] * 2 + core, where[1] * SIDE + where[2])


def shifted(where, axis, d):
    moved = list(where)
    moved[axis] = lax.rem(where[axis] + d, SIDE)
    return tuple(moved)


def pick(fixed, lo, hi):
    return tuple(fixed.get(a, slice(None)) for a in range(3)) + (slice(lo, hi),)


def main_kernel(
    plan_ref,
    mask_in,
    trig_in,
    stacked_in,
    paired_in,
    steer_in,
    scene_ref,
    grad_ref,
    mask,
    omask,
    trig,
    stacked,
    paired,
    steer,
    tiles,
    crecv,
    s1,
    r1a, r1b, r1c,
    s2a, s2b, s2c,
    r2a, r2b, r2c,
    s3a, s3b, s3c,
    r3a, r3b, r3c,
    units,
    wf,
    acc,
    lsem,
    msem,
    csend, crcv,
    s1send, s1recv,
    s2send, s2recv,
    s3send, s3recv,
    gsend, grecv,
    fsend, frecv,
):
    r1, s2, r2, s3, r3 = (r1a, r1b, r1c), (s2a, s2b, s2c), (r2a, r2b, r2c), (s3a, s3b, s3c), (r3a, r3b, r3c)
    where, core = position()
    other = device_at(where, 1 - core)
    pulses = trig.shape[1]
    slots = steer.shape[0]

    local = []
    for n, (src, dst) in enumerate(
        ((mask_in, mask), (trig_in, trig), (stacked_in, stacked), (paired_in, paired))
    ):
        cp = pltpu.make_async_copy(src, dst, lsem.at[slots + n])
        cp.start()
        local.append(cp)
    for j in range(slots):
        pltpu.make_async_copy(steer_in.at[j], steer.at[j], lsem.at[j]).start()

    barrier = pltpu.get_barrier_semaphore()
    pl.semaphore_signal(barrier, inc=1, device_id=other, device_id_type=MESH)
    for axis in range(3):
        for d in range(1, SIDE):
            pl.semaphore_signal(
                barrier, inc=1, device_id=device_at(shifted(where, axis, d), core), device_id_type=MESH
            )
    local[0].wait()
    local[1].wait()

    def turn(j, carry):
        pltpu.make_async_copy(steer_in.at[j], steer.at[j], lsem.at[j]).wait()
        cosine = trig[0:1, :]
        sines = trig[1:2, :]

        def rows(i, c2):
            at = pl.ds(pl.multiple_of(i * 64, 64), 64)
            re = steer[j, at, :pulses].astype(jnp.float32)
            im = steer[j, at, pulses:].astype(jnp.float32)
            steer[j, at, :pulses] = (re * cosine - im * sines).astype(jnp.bfloat16)
            steer[j, at, pulses:] = (re * sines + im * cosine).astype(jnp.bfloat16)
            return c2

        return lax.fori_loop(0, steer.shape[1] // 64, rows, carry)

    lax.fori_loop(0, slots, turn, 0)

    pl.semaphore_wait(barrier, 10)
    mcopy = pltpu.make_async_remote_copy(
        src_ref=mask, dst_ref=omask, send_sem=msem.at[0], recv_sem=msem.at[1], device_id=other, device_id_type=MESH
    )
    mcopy.start()
    local[2].wait()
    local[3].wait()

    def core_copy(t):
        return pltpu.make_async_remote_copy(
            src_ref=tiles.at[t, :, 1 - core],
            dst_ref=crecv.at[t],
            send_sem=csend.at[t],
            recv_sem=crcv.at[t],
            device_id=other,
            device_id_type=MESH,
        )

    stage1 = []

    def send1(p, d, sub, src_fixed, sem):
        lo, hi, order = PARTS[p]
        axis = order[0]
        fixed = dict(src_fixed)
        target = shifted(where, axis, d)
        fixed[axis] = target[axis]
        rest = tuple(a for a in range(3) if a != axis)
        dst = tuple(src_fixed.get(a, slice(None)) for a in rest)
        cp = pltpu.make_async_remote_copy(
            src_ref=s1.at[pick(fixed, lo, hi)],
            dst_ref=r1[p].at[(d - 1,) + dst],
            send_sem=s1send.at[sem],
            recv_sem=s1recv.at[sem],
            device_id=device_at(target, core),
            device_id_type=MESH,
        )
        cp.start()
        return cp

    for g in range(SIDE):
        z = lax.rem(where[1] + 1 + g, SIDE)

        def compute(x, carry):
            t = z * SIDE + x
            left = steer[plan_ref[0, t]]
            right = stacked[plan_ref[1, t]]
            part = jnp.dot(left, right, preferred_element_type=jnp.float32)
            tiles[t] = part.reshape(tiles.shape[1:])
            core_copy(t).start()
            return carry

        lax.fori_loop(0, SIDE, compute, 0)
        if g == 0:
            mcopy.wait()

        def combine(x, carry):
            t = z * SIDE + x
            core_copy(t).wait_recv()
            for k in range(2):
                m = mask[pl.ds(t * 2 + k, 1), :]
                om = omask[pl.ds(t * 2 + k, 1), :]
                for lg in range(4):
                    lanes = slice(lg * LANE, (lg + 1) * LANE)
                    for y in range(SIDE):
                        v = tiles[t, y, core, :, lanes] * m + crecv[t, y, :, lanes] * om
                        u = k * 8 + lg * 2
                        s1[y, z, x, u : u + 2] = v.astype(jnp.bfloat16).reshape(2, SUB, LANE)
            return carry

        lax.fori_loop(0, SIDE, combine, 0)
        for d in range(1, SIDE):
            stage1.append(send1(0, d, g, {1: z}, g * 6 + d - 1))
            stage1.append(send1(2, d, g, {1: z}, g * 6 + 3 + d - 1))
        if g < SIDE - 1:
            stage1.append(send1(1, g + 1, 0, {}, 24 + g))

    def all_core(t, carry):
        core_copy(t).wait_send()
        return carry

    for cp in stage1:
        cp.wait_recv()

    stage2 = []
    for p, (lo, hi, order) in enumerate(PARTS):
        a, b, _ = order
        rest = [x for x in range(3) if x != a]
        bpos = rest.index(b)

        def add(i, carry):
            o = lax.rem(i, SIDE)
            q = i // SIDE
            fixed = {a: where[a], rest[0]: q, rest[1]: o}
            v = s1[pick(fixed, lo, hi)].astype(jnp.float32)
            for d in range(SIDE - 1):
                v = v + r1[p][d, q, o].astype(jnp.float32)
            s2[p][q, o] = v
            return carry

        lax.fori_loop(0, SIDE * SIDE, add, 0)
        for d in range(1, SIDE):
            target = shifted(where, b, d)
            idx = (target[b],) if bpos == 0 else (slice(None), target[b])
            cp = pltpu.make_async_remote_copy(
                src_ref=s2[p].at[idx],
                dst_ref=r2[p].at[d - 1],
                send_sem=s2send.at[p * 3 + d - 1],
                recv_sem=s2recv.at[p * 3 + d - 1],
                device_id=device_at(target, core),
                device_id_type=MESH,
            )
            cp.start()
            stage2.append(cp)

    stage3 = []
    for p, (lo, hi, order) in enumerate(PARTS):
        a, b, c = order
        rest = [x for x in range(3) if x != a]
        bpos = rest.index(b)
        for cp in stage2[p * 3 : p * 3 + 3]:
            cp.wait_recv()
        for q in range(SIDE):
            v = s2[p][where[b], q] if bpos == 0 else s2[p][q, where[b]]
            for d in range(SIDE - 1):
                v = v + r2[p][d, q]
            s3[p][q] = v
        for d in range(1, SIDE):
            target = shifted(where, c, d)
            cp = pltpu.make_async_remote_copy(
                src_ref=s3[p].at[target[c]],
                dst_ref=r3[p].at[d - 1],
                send_sem=s3send.at[p * 3 + d - 1],
                recv_sem=s3recv.at[p * 3 + d - 1],
                device_id=device_at(target, core),
                device_id_type=MESH,
            )
            cp.start()
            stage3.append(cp)

    for p, (lo, hi, order) in enumerate(PARTS):
        for cp in stage3[p * 3 : p * 3 + 3]:
            cp.wait_recv()
        v = s3[p][where[order[2]]]
        for d in range(SIDE - 1):
            v = v + r3[p][d]
        units[lo:hi] = v

    y0, z0, x0 = where
    for k in range(2):
        for lg in range(2):
            for rh in range(2):
                ur = k * 8 + lg * 2 + rh
                re = units[ur]
                im = units[ur + 4]
                power = re * re + im * im
                wf[core, y0, z0, x0, ur] = (re * power).astype(jnp.bfloat16)
                wf[core, y0, z0, x0, ur + 4] = (im * power).astype(jnp.bfloat16)
                rows = slice(rh * SUB, (rh + 1) * SUB)
                scene_ref[k, rows, lg * LANE : (lg + 1) * LANE] = re
                scene_ref[k, rows, (lg + 2) * LANE : (lg + 3) * LANE] = im

    done = []

    def gather(p, step):
        lo, hi, order = PARTS[p]
        axis = order[2 - step]
        keep = order[: 3 - step]
        fixed = {a: where[a] for a in keep}
        src = wf.at[(core,) + pick(fixed, lo, hi)]
        out = []
        for d in range(1, SIDE):
            n = (step * 3 + p) * 3 + d - 1
            cp = pltpu.make_async_remote_copy(
                src_ref=src,
                dst_ref=src,
                send_sem=gsend.at[n],
                recv_sem=grecv.at[n],
                device_id=device_at(shifted(where, axis, d), core),
                device_id_type=MESH,
            )
            cp.start()
            out.append(cp)
        return out

    def forward(p, step, d):
        lo, hi, order = PARTS[p]
        axis = order[2 - step]
        keep = order[: 3 - step]
        fixed = {a: where[a] for a in keep}
        fixed[axis] = lax.rem(where[axis] + SIDE - d, SIDE)
        src = wf.at[(core,) + pick(fixed, lo, hi)]
        n = (step * 3 + p) * 4 + d
        cp = pltpu.make_async_remote_copy(
            src_ref=src,
            dst_ref=src,
            send_sem=fsend.at[n],
            recv_sem=frecv.at[n],
            device_id=other,
            device_id_type=MESH,
        )
        cp.start()
        return cp

    gathers = {}
    forwards = []
    for p in range(3):
        gathers[p] = gather(p, 0)
        forwards.append(forward(p, 0, 0))
    for step in range(3):
        for p in range(3):
            current = gathers[p]
            for d in range(1, SIDE):
                current[d - 1].wait_recv()
                forwards.append(forward(p, step, d))
            done.extend(current)
            if step < 2:
                gathers[p] = gather(p, step + 1)
    for cp in forwards:
        cp.wait_recv()

    acc[...] = jnp.zeros_like(acc)

    def backward(j, carry):
        zj = plan_ref[2, j]
        xj = plan_ref[3, j]
        kj = plan_ref[4, j]
        live = jnp.where(plan_ref[5, j] > 0, jnp.float32(1.0), jnp.float32(0.0))
        groups = []
        for lg in range(4):
            pieces = [
                wf[c, y, zj, xj, pl.ds(kj * 8 + lg * 2, 2)].reshape(2 * SUB, LANE)
                for y in range(SIDE)
                for c in range(2)
            ]
            groups.append(jnp.concatenate(pieces, axis=0))
        weight = jnp.concatenate(groups, axis=1)
        moments = lax.dot_general(
            weight, paired[kj], (((1,), (1,)), ((), ())), preferred_element_type=jnp.float32
        )
        re = steer[j, :, :pulses].astype(jnp.float32)
        im = steer[j, :, pulses:].astype(jnp.float32)
        term = re * moments[:, pulses:] + im * moments[:, :pulses]
        acc[...] += jnp.sum(term.reshape(-1, 8, pulses), axis=0) * live
        return carry

    lax.fori_loop(0, slots, backward, 0)
    factor = -4.0 / math.sqrt(steer.shape[1] * (stacked.shape[2] // 2))
    grad_ref[...] = jnp.sum(acc[...], axis=0, keepdims=True) * factor

    lax.fori_loop(0, 4 * SIDE, all_core, 0)
    for cp in stage1 + stage2 + stage3 + done + forwards:
        cp.wait_send()


def on_device(echoes, phases, kernel, steering, footprint, counts, range_start):
    columns = lax.axis_size("tile")
    row_parts = lax.axis_size("pulse")
    pulses = echoes.shape[0]
    window_len = kernel.shape[1]
    breadth = kernel.shape[2]
    height = steering.shape[2]
    slots = steering.shape[1]
    tile_rows = range_start.shape[1]
    part_rows = height // row_parts
    width = 2 * breadth
    ids = footprint[0]
    used = jnp.arange(slots, dtype=jnp.int32) < counts[0]
    hit = (ids[None, :] % columns == jnp.arange(columns, dtype=jnp.int32)[:, None]) & used[None, :]
    slot_of = jnp.sum(jnp.where(hit, jnp.arange(slots, dtype=jnp.int32)[None, :], 0), axis=1)
    label = jnp.sum(jnp.where(hit, ids[None, :] // columns + 1, 0), axis=1) - 1
    pad = lambda v: jnp.pad(v, (0, columns - slots))
    plan = jnp.stack(
        [
            slot_of,
            jnp.maximum(label, 0),
            pad(ids % columns // SIDE),
            pad(ids % SIDE),
            pad(ids // columns),
            pad(used.astype(jnp.int32)),
        ]
    )
    mask = (label[:, None] == jnp.arange(tile_rows)[None, :]).astype(jnp.float32).reshape(-1, 1)
    mask = jnp.broadcast_to(mask, (columns * tile_rows, LANE))
    trig = jnp.stack([jnp.cos(phases), jnp.sin(phases)])
    stacked, paired = [], []
    for k in range(tile_rows):
        window = lax.dynamic_slice_in_dim(echoes, range_start[0, k], window_len, 2)
        prof = (
            jnp.dot(window.reshape(2 * pulses, window_len), kernel[0], preferred_element_type=jnp.float32)
            .astype(jnp.bfloat16)
            .reshape(pulses, width)
        )
        re, im = prof[:, :breadth], prof[:, breadth:]
        stacked.append(jnp.concatenate([prof, jnp.concatenate([-im, re], axis=1)], axis=0))
        paired.append(jnp.concatenate([prof, jnp.concatenate([im, -re], axis=1)], axis=0))
    stacked, paired = jnp.stack(stacked), jnp.stack(paired)

    f32, bf16 = jnp.float32, jnp.bfloat16
    sizes = [hi - lo for lo, hi, _ in PARTS]
    vmem = pltpu.VMEM
    sem = lambda n: pltpu.SemaphoreType.DMA((n,))
    anywhere = pl.BlockSpec(memory_space=pl.ANY)
    scene, grad = pl.pallas_call(
        main_kernel,
        out_shape=(
            jax.ShapeDtypeStruct((tile_rows, part_rows, width), f32),
            jax.ShapeDtypeStruct((1, pulses), f32),
        ),
        in_specs=[pl.BlockSpec(memory_space=pltpu.SMEM)] + [anywhere] * 5,
        out_specs=[pl.BlockSpec(memory_space=pltpu.VMEM)] * 2,
        scratch_shapes=[
            vmem(mask.shape, f32),
            vmem(mask.shape, f32),
            vmem(trig.shape, f32),
            vmem(stacked.shape, bf16),
            vmem(paired.shape, bf16),
            vmem((slots, height, 2 * pulses), bf16),
            vmem((columns, SIDE, 2, part_rows, width), f32),
            vmem((columns, SIDE, part_rows, width), f32),
            vmem((SIDE, SIDE, SIDE, 16, SUB, LANE), bf16),
        ]
        + [vmem((3, SIDE, SIDE, n, SUB, LANE), bf16) for n in sizes]
        + [vmem((SIDE, SIDE, n, SUB, LANE), f32) for n in sizes]
        + [vmem((3, SIDE, n, SUB, LANE), f32) for n in sizes]
        + [vmem((SIDE, n, SUB, LANE), f32) for n in sizes]
        + [vmem((3, n, SUB, LANE), f32) for n in sizes]
        + [
            vmem((16, SUB, LANE), f32),
            vmem((2, SIDE, SIDE, SIDE, 16, SUB, LANE), bf16),
            vmem((8, pulses), f32),
            sem(slots + 4),
            sem(2),
            sem(columns), sem(columns),
            sem(27), sem(27),
            sem(9), sem(9),
            sem(9), sem(9),
            sem(27), sem(27),
            sem(36), sem(36),
        ],
        compiler_params=pltpu.CompilerParams(
            collective_id=0, has_side_effects=True, vmem_limit_bytes=60 << 20
        ),
    )(plan, mask, trig, stacked, paired, steering[0])
    return (scene[:, None], grad[0])


def solution(mesh):
    placed = (
        P(("pulse", "tile"), None, None),
        P(("pulse", "tile")),
        P(("pulse", "tile"), None, None),
        P(("pulse", "tile"), None, None, None),
        P(("pulse", "tile"), None),
        P(("pulse", "tile")),
        P(("pulse", "tile"), None),
    )
    return jax.shard_map(
        on_device,
        mesh=mesh,
        in_specs=placed,
        out_specs=(P(None, "tile", "pulse", None), P(("pulse", "tile"))),
        check_vma=False,
    )
```

time: 650 us -> 109 us (0.17)
  the two profiles are of different devices: /device:TPU:41 before, /device:TPU:1 now
where the time goes in v1:
time: 109 us
  Pallas kernels  90 us (83%)
  local copies, waits for them, and re-layouts  9.39 us (9%)
  between operations  5.32 us (5%)
  other arithmetic  3.62 us (3%)
    pallas_call x1, Pallas kernels, on_device(): pl.pallas_call(main_kernel, out_shape=(jax.ShapeDtypeStruct((tile_rows, p...  90 us
    dynamic_slice x1, local copies, waits for them, and re-layouts, on_device(): window = lax.dynamic_slice_in_dim(echoes, range_start[0, k], window_len, 2)  3.07 us
    unnamed x8, local copies, waits for them, and re-layouts  2.84 us
    another operation x3, other arithmetic, on_device(): stacked, paired = (jnp.stack(stacked), jnp.stack(paired))  2.64 us

profile of v1, /device:TPU:1, one launch (start us, length us, event | category | flops | bytes accessed | tf_op | source)
XLA Modules:
  0.0 108.9 jit_solution(3020562747286606372)
XLA Ops:
  0.6 0.0 copy-start
  0.6 1.3 %fusion.13 = (s32[1,1]{1,0:T(1,128)}, s32[1,1]{1,0:T(1,128)}) fusion(s32[1,2]{1,0:T(1,128)} %param.13), kind=kLoop, calls=%fused_computation.58 | loop fusion | bytes 16 | tf_op jit(solution)/shard_map/slice | solution.py:406
  5.8 3.1 %constant_dynamic-slice_fusion = (bf16[512,2,256]{2,1,0:T(2,128)(2,1)S(1)}, bf16[512,2,256]{2,1,0:T(2,128)(2,1)S(1)}) fusion(bf16[512,2,4096]{2,1,0:T(2,128)(2,1)} %param.7, s32[]{:T(128)S(6)} %select_n.51, s32[]{:T(128)S(6)} %select_n.52), kind=kLoop, calls=%fused_computation.48 | loop fusion | bytes 2097160 | tf_op jit(solution)/shard_map/dynamic_slice | solution.py:406
  8.9 0.2 reshape.55
  9.1 0.0 copy-done
  9.1 0.3 convolution_convert_fusion.1
  9.4 0.2 reshape.56
  9.6 0.1 fusion.10
  9.7 0.2 fusion.3
  9.8 0.2 reshape.57
  10.1 0.3 convolution_convert_fusion
  10.4 0.2 reshape.58
  10.5 0.1 fusion.11
  10.6 0.2 fusion.1
  10.8 0.0 copy-start.2
  10.8 0.0 copy-start.1
  10.8 2.3 %pad_maximum_fusion = (bf16[2,1024,512]{2,1,0:T(8,128)(2,1)}, bf16[2,1024,512]{2,1,0:T(8,128)(2,1)}) fusion(bf16[1,1024,512]{2,1,0:T(8,128)(2,1)S(1)} %get-tuple-element.23, bf16[1,1024,512]{2,1,0:T(8,128)(2,1)S(1)} %get-tuple-element.17, bf16[1,1024,512]{2,1,0:T(8,128)(2,1)S(1)} %get-tuple-element.22, bf16[1,1024,512]{2,1,0:T(8,128)(2,1)S(1)} %get-tuple-element.16), kind=kLoop, calls=%fused_computation | loop fusion | flops 2097152 | bytes 8388608 | tf_op jit(solution)/shard_map/stack | solution.py:415
  13.1 0.0 copy-done.2
  13.8 0.1 select_reduce_fusion
  14.0 0.6 stack.55.plan_ref
  14.6 0.1 fusion.7
  14.7 0.1 reshape.60
  14.8 0.7 broadcast_in_dim.37.mask_in
  15.4 0.0 copy-done.1
  15.5 0.6 pad_maximum_fusion.6.trig_in
  16.1 90.0 %shard_map.86 = (f32[2,32,512]{2,1,0:T(8,128)}, f32[1,512]{1,0:T(1,128)}) custom-call(s32[6,16]{1,0:T(8,128)} %stack.55.plan_ref, f32[32,128]{1,0:T(8,128)} %broadcast_in_dim.37.mask_in, f32[2,512]{1,0:T(2,128)} %pad_maximum_fusion.6.trig_in, bf16[2,1024,512]{2,1,0:T(8,128)(2,1)} %get-tuple-element.41.stacked_in, ...), custom_call_target="tpu_custom_call" | custom-call | tf_op jit(solution)/shard_map/pallas_call | solution.py:422
  106.1 1.6 %copy.15 = f32[2,1,32,512]{3,2,1,0:T(8,128)} copy(f32[2,1,32,512]{3,2,1,0:T(8,128)} %bitcast.66) | data formatting | bytes 262144
  107.7 1.3 %copy.16 = f32[512]{0:T(512)} copy(f32[512]{0:T(512)} %bitcast.70) | data formatting | bytes 4096
  (8 shorter events, 0.1 us)
Async XLA Ops:
  0.6 8.5 %copy-start = (bf16[1,256,256]{2,1,0:T(8,128)(2,1)S(1)}, bf16[1,256,256]{2,1,0:T(8,128)(2,1)}, u32[]{:S(2)}) copy-start(bf16[1,256,256]{2,1,0:T(8,128)(2,1)} %param.9) | copy-start | bytes 393220
  10.8 2.4 %copy-start.2 = (s32[1,12]{1,0:T(1,128)S(1)}, s32[1,12]{1,0:T(1,128)}, u32[]{:S(2)}) copy-start(s32[1,12]{1,0:T(1,128)} %param.11) | copy-start | bytes 148
  10.8 4.7 %copy-start.1 = (f32[512]{0:T(512)S(1)}, f32[512]{0:T(512)}, u32[]{:S(2)}) copy-start(f32[512]{0:T(512)} %param.8) | copy-start | bytes 6148

commit v2 on v1

v2 whole, which is shorter than its diff:
```python
import functools
import math

import jax
import jax.numpy as jnp
from jax import lax
from jax.experimental import pallas as pl
from jax.experimental.pallas import tpu as pltpu
from jax.sharding import PartitionSpec as P

MESH = pl.DeviceIdType.MESH
SIDE = 4
LANE = 128
SUB = 16
PARTS = (
    (0, 6, (0, 1, 2)),
    (6, 10, (1, 2, 0)),
    (10, 16, (2, 1, 0)),
)
NEAR_FIRST = (1, 3, 2)


def position():
    p = lax.axis_index("pulse")
    t = lax.axis_index("tile")
    core = p % 2
    return turned((p // 2, t // SIDE, t % SIDE), core), core


def turned(place, core):
    first = jnp.where(core == 0, place[0], place[2])
    last = jnp.where(core == 0, place[2], place[0])
    return (first, place[1], last)


def device_at(where, core):
    y, z, x = turned(where, core)
    return (y * 2 + core, z * SIDE + x)


def shifted(where, axis, d):
    moved = list(where)
    moved[axis] = lax.rem(where[axis] + d, SIDE)
    return tuple(moved)


def pick(fixed, lo, hi):
    return tuple(fixed.get(a, slice(None)) for a in range(3)) + (slice(lo, hi),)


def local_kernel(
    foot_ref,
    count_ref,
    start_ref,
    phases_ref,
    kernel_ref,
    echoes_in,
    plan_ref,
    mask,
    trig,
    stacked,
    windows,
    raw,
    sem,
):
    pulses = phases_ref.shape[1]
    window_len, breadth = kernel_ref.shape
    span = window_len + LANE
    last = (echoes_in.shape[2] - span) // LANE
    slots = foot_ref.shape[1]
    blocks = [jnp.minimum(start_ref[0, k] // LANE, last) for k in range(2)]
    copies = []
    for k in range(2):
        cp = pltpu.make_async_copy(
            echoes_in.at[:, :, pl.ds(pl.multiple_of(blocks[k] * LANE, LANE), span)], windows.at[k], sem.at[k]
        )
        cp.start()
        copies.append(cp)
    count = count_ref[0]
    for t in range(SIDE * SIDE):
        for n in range(6):
            plan_ref[n, t] = jnp.int32(0)
    tile_id = lax.broadcasted_iota(jnp.int32, mask.shape, 0)
    tile_id = tile_id // 2 + tile_id % 2 * (SIDE * SIDE)
    found = jnp.zeros(mask.shape, jnp.float32)
    for j in range(slots):
        name = foot_ref[0, j]
        live = j < count
        found = jnp.where(tile_id == jnp.where(live, name, -1), jnp.float32(1.0), found)
        plan_ref[2, j] = name // SIDE % SIDE
        plan_ref[3, j] = name % SIDE
        plan_ref[4, j] = name // (SIDE * SIDE)
        plan_ref[5, j] = live.astype(jnp.int32)

        @pl.when(live)
        def _():
            t = name % (SIDE * SIDE)
            plan_ref[0, t] = jnp.int32(j)
            plan_ref[1, t] = name // (SIDE * SIDE)

    mask[...] = found
    angle = phases_ref[...]
    trig[0:1, :] = jnp.cos(angle)
    trig[1:2, :] = jnp.sin(angle)
    depth = pulses // SIDE
    for k in range(2):
        weights = jnp.concatenate(
            [kernel_ref[...].astype(jnp.float32), jnp.zeros((LANE, breadth), jnp.float32)], axis=0
        )
        weights = pltpu.roll(weights, start_ref[0, k] - blocks[k] * LANE, 0).astype(jnp.bfloat16)
        copies[k].wait()

        def interpolate(i, carry):
            at = pl.multiple_of(i * depth, depth)
            window = windows[k, pl.ds(at, depth)]
            value = jnp.dot(window.reshape(2 * depth, span), weights, preferred_element_type=jnp.float32)
            top, low = pl.ds(at, depth), pl.ds(pulses + at, depth)
            for h in range(breadth // LANE):
                raw[h] = value[:, h * LANE : (h + 1) * LANE]
                re = raw[h, pl.ds(0, depth, stride=2), :].astype(jnp.bfloat16)
                im = raw[h, pl.ds(1, depth, stride=2), :].astype(jnp.bfloat16)
                left = slice(h * LANE, (h + 1) * LANE)
                right = slice(breadth + h * LANE, breadth + (h + 1) * LANE)
                stacked[k, top, left] = re
                stacked[k, top, right] = im
                stacked[k, low, left] = -im
                stacked[k, low, right] = re
            return carry

        lax.fori_loop(0, SIDE, interpolate, 0)


def main_kernel(
    plan_ref,
    mask_in,
    trig_in,
    stacked_in,
    steer_in,
    scene_ref,
    grad_ref,
    mask,
    omask,
    trig,
    stacked,
    steer,
    tiles,
    crecv,
    s1,
    r1a, r1b, r1c,
    s2a, s2b, s2c,
    r2a, r2b, r2c,
    s3a, s3b, s3c,
    r3a, r3b, r3c,
    units,
    wf,
    acc,
    lsem,
    msem,
    csend, crcv,
    s1send, s1recv,
    s2send, s2recv,
    s3send, s3recv,
    gsend, grecv,
    fsend, frecv,
):
    r1, s2, r2, s3, r3 = (r1a, r1b, r1c), (s2a, s2b, s2c), (r2a, r2b, r2c), (s3a, s3b, s3c), (r3a, r3b, r3c)
    where, core = position()
    y_own, z_own, x_own = turned(where, core)
    other = (y_own * 2 + 1 - core, z_own * SIDE + x_own)
    pulses = trig.shape[1]
    slots = steer.shape[0]

    for j in range(slots):
        pltpu.make_async_copy(steer_in.at[j], steer.at[j], lsem.at[j]).start()
    local = []
    for n, (src, dst) in enumerate(((mask_in, mask), (trig_in, trig), (stacked_in, stacked))):
        cp = pltpu.make_async_copy(src, dst, lsem.at[slots + n])
        cp.start()
        local.append(cp)

    barrier = pltpu.get_barrier_semaphore()
    pl.semaphore_signal(barrier, inc=1, device_id=other, device_id_type=MESH)
    for axis in range(3):
        for d in range(1, SIDE):
            pl.semaphore_signal(
                barrier, inc=1, device_id=device_at(shifted(where, axis, d), core), device_id_type=MESH
            )
    local[0].wait()
    local[1].wait()

    def turn(j, carry):
        pltpu.make_async_copy(steer_in.at[j], steer.at[j], lsem.at[j]).wait()
        cosine = trig[0:1, :]
        sines = trig[1:2, :]

        def rows(i, c2):
            at = pl.ds(pl.multiple_of(i * 64, 64), 64)
            re = steer[j, at, :pulses].astype(jnp.float32)
            im = steer[j, at, pulses:].astype(jnp.float32)
            steer[j, at, :pulses] = (re * cosine - im * sines).astype(jnp.bfloat16)
            steer[j, at, pulses:] = (re * sines + im * cosine).astype(jnp.bfloat16)
            return c2

        return lax.fori_loop(0, steer.shape[1] // 64, rows, carry)

    lax.fori_loop(0, slots, turn, 0)

    pl.semaphore_wait(barrier, 10)
    mcopy = pltpu.make_async_remote_copy(
        src_ref=mask, dst_ref=omask, send_sem=msem.at[0], recv_sem=msem.at[1], device_id=other, device_id_type=MESH
    )
    mcopy.start()
    local[2].wait()

    def core_copy(t):
        return pltpu.make_async_remote_copy(
            src_ref=tiles.at[t, :, 1 - core],
            dst_ref=crecv.at[t],
            send_sem=csend.at[t],
            recv_sem=crcv.at[t],
            device_id=other,
            device_id_type=MESH,
        )

    stage1, stage2, stage3 = {}, {}, {}

    def send1(p, d, src_fixed, key):
        lo, hi, order = PARTS[p]
        axis = order[0]
        fixed = dict(src_fixed)
        target = shifted(where, axis, d)
        fixed[axis] = target[axis]
        dst = tuple(src_fixed.get(a, slice(None)) for a in range(3) if a != axis)
        n = len(stage1)
        cp = pltpu.make_async_remote_copy(
            src_ref=s1.at[pick(fixed, lo, hi)],
            dst_ref=r1[p].at[(d - 1,) + dst],
            send_sem=s1send.at[n],
            recv_sem=s1recv.at[n],
            device_id=device_at(target, core),
            device_id_type=MESH,
        )
        cp.start()
        stage1[key] = cp

    def rest_index(p, fixed):
        return tuple(fixed.get(a, slice(None)) for a in range(3) if a != PARTS[p][2][0])

    def add_row(p, row):
        lo, hi, (a, b, c) = PARTS[p]

        def add(o, carry):
            here = rest_index(p, {b: row, c: o})
            v = s1[pick({a: where[a], b: row, c: o}, lo, hi)].astype(jnp.float32)
            for d in range(SIDE - 1):
                v = v + r1[p][(d,) + here].astype(jnp.float32)
            s2[p][here] = v.astype(jnp.bfloat16)
            return carry

        lax.fori_loop(0, SIDE, add, 0)

    def send2(p, d):
        b = PARTS[p][2][1]
        target = shifted(where, b, d)
        cp = pltpu.make_async_remote_copy(
            src_ref=s2[p].at[rest_index(p, {b: target[b]})],
            dst_ref=r2[p].at[d - 1],
            send_sem=s2send.at[p * 3 + d - 1],
            recv_sem=s2recv.at[p * 3 + d - 1],
            device_id=device_at(target, core),
            device_id_type=MESH,
        )
        cp.start()
        stage2[p, d] = cp

    def row_done(p, g):
        for d in NEAR_FIRST:
            stage1[p, g, d].wait_recv()
        add_row(p, lax.rem(where[1] + 1 + g, SIDE))
        if g < SIDE - 1:
            send2(p, g + 1)

    def send3(p):
        lo, hi, (a, b, c) = PARTS[p]
        for d in NEAR_FIRST:
            stage2[p, d].wait_recv()
        for q in range(SIDE):
            v = s2[p][rest_index(p, {b: where[b], c: q})].astype(jnp.float32)
            for d in range(SIDE - 1):
                v = v + r2[p][d, q].astype(jnp.float32)
            s3[p][q] = v
        for d in NEAR_FIRST:
            target = shifted(where, c, d)
            cp = pltpu.make_async_remote_copy(
                src_ref=s3[p].at[target[c]],
                dst_ref=r3[p].at[d - 1],
                send_sem=s3send.at[p * 3 + d - 1],
                recv_sem=s3recv.at[p * 3 + d - 1],
                device_id=device_at(target, core),
                device_id_type=MESH,
            )
            cp.start()
            stage3[p, d] = cp

    for g in range(SIDE):
        z = lax.rem(where[1] + 1 + g, SIDE)

        def compute(x, carry):
            t = z * SIDE + x
            left = steer[plan_ref[0, t]]
            right = stacked[plan_ref[1, t]]
            part = jnp.dot(left, right, preferred_element_type=jnp.float32)
            tiles[t] = part.reshape(tiles.shape[1:])
            core_copy(t).start()
            return carry

        lax.fori_loop(0, SIDE, compute, 0)
        if g == 0:
            mcopy.wait()

        def combine(x, carry):
            t = z * SIDE + x
            core_copy(t).wait_recv()
            for k in range(2):
                m = mask[pl.ds(t * 2 + k, 1), :]
                om = omask[pl.ds(t * 2 + k, 1), :]
                for lg in range(4):
                    lanes = slice(lg * LANE, (lg + 1) * LANE)
                    for y in range(SIDE):
                        v = tiles[t, y, core, :, lanes] * m + crecv[t, y, :, lanes] * om
                        u = k * 8 + lg * 2
                        s1[turned((y, z, x), core) + (slice(u, u + 2),)] = v.astype(jnp.bfloat16).reshape(2, SUB, LANE)
            return carry

        lax.fori_loop(0, SIDE, combine, 0)
        for d in NEAR_FIRST:
            send1(0, d, {1: z}, (0, g, d))
            send1(2, d, {1: z}, (2, g, d))
        if g < SIDE - 1:
            send1(1, g + 1, {}, (1, g + 1))

    def all_core(t, carry):
        core_copy(t).wait_send()
        return carry

    for g in range(2):
        row_done(0, g)
        row_done(2, g)
    for d in NEAR_FIRST:
        stage1[1, d].wait_recv()
    for d in NEAR_FIRST:
        add_row(1, lax.rem(where[2] + d, SIDE))
        send2(1, d)
    add_row(1, where[2])
    row_done(0, 2)
    row_done(2, 2)
    send3(1)
    row_done(0, 3)
    send3(0)
    row_done(2, 3)
    send3(2)
    for p in (1, 0, 2):
        lo, hi, order = PARTS[p]
        v = s3[p][where[order[2]]]
        for d in range(1, SIDE):
            stage3[p, d].wait_recv()
            v = v + r3[p][d - 1]
        units[lo:hi] = v

    for k in range(2):
        for lg in range(2):
            for rh in range(2):
                ur = k * 8 + lg * 2 + rh
                re = units[ur]
                im = units[ur + 4]
                power = re * re + im * im
                wf[(core,) + where + (ur,)] = (re * power).astype(jnp.bfloat16)
                wf[(core,) + where + (ur + 4,)] = (im * power).astype(jnp.bfloat16)
                rows = slice(rh * SUB, (rh + 1) * SUB)
                scene_ref[k, rows, lg * LANE : (lg + 1) * LANE] = re
                scene_ref[k, rows, (lg + 2) * LANE : (lg + 3) * LANE] = im

    gathers, forwards = {}, []

    def gather(p, fixed, axis, d, key):
        lo, hi, _ = PARTS[p]
        src = wf.at[(core,) + pick(fixed, lo, hi)]
        n = len(gathers)
        cp = pltpu.make_async_remote_copy(
            src_ref=src,
            dst_ref=src,
            send_sem=gsend.at[n],
            recv_sem=grecv.at[n],
            device_id=device_at(shifted(where, axis, d), core),
            device_id_type=MESH,
        )
        cp.start()
        gathers[key] = cp

    def forward(p, fixed):
        lo, hi, _ = PARTS[p]
        src = wf.at[(core,) + pick(fixed, lo, hi)]
        n = len(forwards)
        cp = pltpu.make_async_remote_copy(
            src_ref=src,
            dst_ref=src,
            send_sem=fsend.at[n],
            recv_sem=frecv.at[n],
            device_id=other,
            device_id_type=MESH,
        )
        cp.start()
        forwards.append(cp)

    def back(axis, d):
        return lax.rem(where[axis] + SIDE - d, SIDE)

    order_of = (0, 2, 1)
    for p in order_of:
        for d in NEAR_FIRST:
            gather(p, dict(enumerate(where)), PARTS[p][2][2], d, (p, "c", d))

    def row_out(p, r):
        a, b, c = PARTS[p][2]
        row = {a: where[a], b: back(b, r)}
        for d in (1, 3):
            gather(p, row, a, d, (p, r, d))
        forward(p, row)

    for p in order_of:
        a, b, c = PARTS[p][2]
        for d in NEAR_FIRST:
            gathers[p, "c", d].wait_recv()
        for d in NEAR_FIRST:
            gather(p, {a: where[a], b: where[b]}, b, d, (p, "b", d))
        row_out(p, 0)
    for d in NEAR_FIRST:
        for p in order_of:
            gathers[p, "b", d].wait_recv()
            row_out(p, d)
    rows_in = (0,) + NEAR_FIRST
    for r in rows_in:
        for p in order_of:
            a, b, c = PARTS[p][2]
            for d, half in ((1, slice(0, 2)), (3, slice(2, 4))):
                gathers[p, r, d].wait_recv()
                gather(p, {a: back(a, d), b: back(b, r), c: half}, a, d, (p, r, "far", d))
                forward(p, {a: back(a, d), b: back(b, r)})
    for r in rows_in:
        for p in order_of:
            a, b, c = PARTS[p][2]
            for d, half in ((1, slice(0, 2)), (3, slice(2, 4))):
                gathers[p, r, "far", d].wait_recv()
                forward(p, {a: back(a, 2), b: back(b, r), c: half})
    for cp in forwards:
        cp.wait_recv()

    acc[...] = jnp.zeros_like(acc)

    def backward(j, carry):
        zj = plan_ref[2, j]
        xj = plan_ref[3, j]
        kj = plan_ref[4, j]
        live = jnp.where(plan_ref[5, j] > 0, jnp.float32(1.0), jnp.float32(0.0))
        groups = []
        for lg in range(4):
            pieces = [
                wf[((c,) + ((y, zj, xj) if c == 0 else (xj, zj, y))) + (pl.ds(kj * 8 + lg * 2, 2),)].reshape(2 * SUB, LANE)
                for y in range(SIDE)
                for c in range(2)
            ]
            groups.append(jnp.concatenate(pieces, axis=0))
        weight = jnp.concatenate(groups, axis=1)
        moments = lax.dot_general(
            weight, stacked[kj], (((1,), (1,)), ((), ())), preferred_element_type=jnp.float32
        )
        re = steer[j, :, :pulses].astype(jnp.float32)
        im = steer[j, :, pulses:].astype(jnp.float32)
        term = im * moments[:, :pulses] - re * moments[:, pulses:]
        acc[...] += jnp.sum(term.reshape(-1, 8, pulses), axis=0) * live
        return carry

    lax.fori_loop(0, slots, backward, 0)
    factor = -4.0 / math.sqrt(steer.shape[1] * (stacked.shape[2] // 2))
    grad_ref[...] = jnp.sum(acc[...], axis=0, keepdims=True) * factor

    lax.fori_loop(0, 4 * SIDE, all_core, 0)
    for cp in [*stage1.values(), *stage2.values(), *stage3.values(), *gathers.values(), *forwards]:
        cp.wait_send()


def on_device(echoes, phases, kernel, steering, footprint, counts, range_start):
    columns = lax.axis_size("tile")
    row_parts = lax.axis_size("pulse")
    pulses = echoes.shape[0]
    breadth = kernel.shape[2]
    height = steering.shape[2]
    slots = steering.shape[1]
    tile_rows = range_start.shape[1]
    part_rows = height // row_parts
    width = 2 * breadth

    f32, bf16 = jnp.float32, jnp.bfloat16
    sizes = [hi - lo for lo, hi, _ in PARTS]
    vmem = pltpu.VMEM
    sem = lambda n: pltpu.SemaphoreType.DMA((n,))
    anywhere = pl.BlockSpec(memory_space=pl.ANY)
    smem = pl.BlockSpec(memory_space=pltpu.SMEM)
    whole = pl.BlockSpec(memory_space=pltpu.VMEM)
    span = kernel.shape[1] + LANE
    plan, mask, trig, stacked = pl.pallas_call(
        local_kernel,
        out_shape=(
            jax.ShapeDtypeStruct((6, columns), jnp.int32),
            jax.ShapeDtypeStruct((columns * tile_rows, LANE), f32),
            jax.ShapeDtypeStruct((2, pulses), f32),
            jax.ShapeDtypeStruct((tile_rows, 2 * pulses, width), bf16),
        ),
        in_specs=[smem] * 3 + [whole] * 2 + [anywhere],
        out_specs=[smem] + [whole] * 3,
        scratch_shapes=[
            vmem((tile_rows, pulses, 2, span), bf16),
            vmem((breadth // LANE, 2 * pulses // SIDE, LANE), f32),
            sem(2),
        ],
    )(footprint, counts, range_start, phases[None], kernel[0], echoes)
    scene, grad = pl.pallas_call(
        main_kernel,
        out_shape=(
            jax.ShapeDtypeStruct((tile_rows, part_rows, width), f32),
            jax.ShapeDtypeStruct((1, pulses), f32),
        ),
        in_specs=[smem] + [anywhere] * 4,
        out_specs=[whole] * 2,
        scratch_shapes=[
            vmem((columns * tile_rows, LANE), f32),
            vmem((columns * tile_rows, LANE), f32),
            vmem((2, pulses), f32),
            vmem((tile_rows, 2 * pulses, width), bf16),
            vmem((slots, height, 2 * pulses), bf16),
            vmem((columns, SIDE, 2, part_rows, width), f32),
            vmem((columns, SIDE, part_rows, width), f32),
            vmem((SIDE, SIDE, SIDE, 16, SUB, LANE), bf16),
        ]
        + [vmem((3, SIDE, SIDE, n, SUB, LANE), bf16) for n in sizes]
        + [vmem((SIDE, SIDE, n, SUB, LANE), bf16) for n in sizes]
        + [vmem((3, SIDE, n, SUB, LANE), bf16) for n in sizes]
        + [vmem((SIDE, n, SUB, LANE), f32) for n in sizes]
        + [vmem((3, n, SUB, LANE), f32) for n in sizes]
        + [
            vmem((16, SUB, LANE), f32),
            vmem((2, SIDE, SIDE, SIDE, 16, SUB, LANE), bf16),
            vmem((8, pulses), f32),
            sem(slots + 3),
            sem(2),
            sem(columns), sem(columns),
            sem(27), sem(27),
            sem(9), sem(9),
            sem(9), sem(9),
            sem(66), sem(66),
            sem(60), sem(60),
        ],
        compiler_params=pltpu.CompilerParams(
            collective_id=0, has_side_effects=True, vmem_limit_bytes=60 << 20
        ),
    )(plan, mask, trig, stacked, steering[0])
    return (scene[:, None], grad[0])


def solution(mesh):
    placed = (
        P(("pulse", "tile"), None, None),
        P(("pulse", "tile")),
        P(("pulse", "tile"), None, None),
        P(("pulse", "tile"), None, None, None),
        P(("pulse", "tile"), None),
        P(("pulse", "tile")),
        P(("pulse", "tile"), None),
    )
    return jax.shard_map(
        on_device,
        mesh=mesh,
        in_specs=placed,
        out_specs=(P(None, "tile", "pulse", None), P(("pulse", "tile"))),
        check_vma=False,
    )
```

time: 109 us -> 89.7 us (0.82)
  local copies, waits for them, and re-layouts: 9.39 us -> 2.82 us
  Pallas kernels: 90 us -> 85.3 us
  between operations: 5.32 us -> 1.29 us
  other arithmetic: 3.62 us -> 0 us
    pallas_call x1, Pallas kernels: 90 us -> 79.5 us  [on_device(): pl.pallas_call(main_kernel, out_shape=(jax.ShapeDtypeStruct((tile_rows, p...]
    pallas_call x0 -> x1, Pallas kernels: none -> 5.78 us  [on_device(): pl.pallas_call(local_kernel, out_shape=(jax.ShapeDtypeStruct((6, columns)...]
    another operation x5 -> x0, other arithmetic: 3.25 us -> none  [the longest x3 2.64 us: on_device(): stacked, paired = (jnp.stack(stacked), jnp.stack(paired))]
    dynamic_slice x1 -> x0, local copies, waits for them, and re-layouts: 3.07 us -> none  [on_device(): window = lax.dynamic_slice_in_dim(echoes, range_start[0, k], window_len, 2)]
    slice x1 -> x0, local copies, waits for them, and re-layouts: 1.31 us -> none  [on_device(): window = lax.dynamic_slice_in_dim(echoes, range_start[0, k], window_len, 2)]
    unnamed x8 -> x2, local copies, waits for them, and re-layouts: 2.84 us -> 2.82 us
where the time goes in v2:
time: 89.7 us; the launch traced here: 89.4 us
  Pallas kernels  85.3 us (95%)
  local copies, waits for them, and re-layouts  2.82 us (3%)
  between operations  1.29 us (1%)
    pallas_call x1, Pallas kernels, on_device(): pl.pallas_call(main_kernel, out_shape=(jax.ShapeDtypeStruct((tile_rows, p...  79.5 us
    pallas_call x1, Pallas kernels, on_device(): pl.pallas_call(local_kernel, out_shape=(jax.ShapeDtypeStruct((6, columns)...  5.78 us
    unnamed x2, local copies, waits for them, and re-layouts  2.82 us

profile of v2, /device:TPU:1, one launch (start us, length us, event | category | flops | bytes accessed | tf_op | source)
XLA Modules:
  0.0 89.4 jit_solution(318255938941274590)
XLA Ops:
  1.3 5.8 %shard_map.86 = (s32[6,16]{1,0:T(8,128)}, f32[32,128]{1,0:T(8,128)}, f32[2,512]{1,0:T(2,128)}, bf16[2,1024,512]{2,1,0:T(8,128)(2,1)}) custom-call(s32[1,12]{1,0:T(1,128)} %foot_ref.1, s32[1]{0:T(128)S(6)} %copy.12.count_ref, s32[1,2]{1,0:T(1,128)} %start_ref.1, f32[1,512]{1,0:T(1,128)} %bitcast.10, bf16[256,256]{1,0:T(8,128)(2,1)} %bitcast.8, ...), custom_call_target="tpu_custom_call" | custom-call | tf_op jit(solution)/shard_map/pallas_call | solution.py:511
  7.1 79.5 %shard_map.87 = (f32[2,32,512]{2,1,0:T(8,128)}, f32[1,512]{1,0:T(1,128)}) custom-call(s32[6,16]{1,0:T(8,128)} %get-tuple-element.8.plan_ref, f32[32,128]{1,0:T(8,128)} %get-tuple-element.9.mask_in, f32[2,512]{1,0:T(2,128)} %get-tuple-element.10.trig_in, bf16[2,1024,512]{2,1,0:T(8,128)(2,1)} %get-tuple-element.11.stacked_in, bf16[12,256,1024]{2,1,0:T(8,128)(2,1)} %bitcast.7), custom_call_target="tpu_custom_call" | custom-call | tf_op jit(solution)/shard_map/pallas_call | solution.py:527
  86.6 1.6 %copy.13 = f32[2,1,32,512]{3,2,1,0:T(8,128)} copy(f32[2,1,32,512]{3,2,1,0:T(8,128)} %bitcast.9) | data formatting | bytes 262144
  88.2 1.3 %copy.14 = f32[512]{0:T(512)} copy(f32[512]{0:T(512)} %bitcast.11) | data formatting | bytes 4096

commit v3 on v2

--- a/solution.py
+++ b/solution.py
@@ -17,7 +17,14 @@
     (6, 10, (1, 2, 0)),
     (10, 16, (2, 1, 0)),
 )
+GATHER_PARTS = (
+    (0, 5, (0, 1, 2)),
+    (5, 10, (1, 2, 0)),
+    (10, 16, (2, 0, 1)),
+)
 NEAR_FIRST = (1, 3, 2)
+LAST_ROW = 2
+LAG = 2
 
 
 def position():
@@ -216,7 +223,7 @@
         return pltpu.make_async_remote_copy(
             src_ref=tiles.at[t, :, 1 - core],
             dst_ref=crecv.at[t],
-            send_sem=csend.at[t],
+            send_sem=csend.at[0],
             recv_sem=crcv.at[t],
             device_id=other,
             device_id_type=MESH,
@@ -235,7 +242,7 @@
         cp = pltpu.make_async_remote_copy(
             src_ref=s1.at[pick(fixed, lo, hi)],
             dst_ref=r1[p].at[(d - 1,) + dst],
-            send_sem=s1send.at[n],
+            send_sem=s1send.at[0],
             recv_sem=s1recv.at[n],
             device_id=device_at(target, core),
             device_id_type=MESH,
@@ -265,7 +272,7 @@
         cp = pltpu.make_async_remote_copy(
             src_ref=s2[p].at[rest_index(p, {b: target[b]})],
             dst_ref=r2[p].at[d - 1],
-            send_sem=s2send.at[p * 3 + d - 1],
+            send_sem=s2send.at[0],
             recv_sem=s2recv.at[p * 3 + d - 1],
             device_id=device_at(target, core),
             device_id_type=MESH,
@@ -294,7 +301,7 @@
             cp = pltpu.make_async_remote_copy(
                 src_ref=s3[p].at[target[c]],
                 dst_ref=r3[p].at[d - 1],
-                send_sem=s3send.at[p * 3 + d - 1],
+                send_sem=s3send.at[p],
                 recv_sem=s3recv.at[p * 3 + d - 1],
                 device_id=device_at(target, core),
                 device_id_type=MESH,
@@ -302,46 +309,65 @@
             cp.start()
             stage3[p, d] = cp
 
-    for g in range(SIDE):
+    def column(i):
+        return lax.rem(where[1] + 1 + i // SIDE, SIDE), i % SIDE
+
+    def compute(i):
+        z, x = column(i)
+        t = z * SIDE + x
+        left = steer[plan_ref[0, t]]
+        right = stacked[plan_ref[1, t]]
+        part = jnp.dot(left, right, preferred_element_type=jnp.float32)
+        tiles[t] = part.reshape(tiles.shape[1:])
+        core_copy(t).start()
+
+    def combine(i):
+        z, x = column(i)
+        t = z * SIDE + x
+        core_copy(t).wait_recv()
+        for k in range(2):
+            m = mask[pl.ds(t * 2 + k, 1), :]
+            om = omask[pl.ds(t * 2 + k, 1), :]
+            for lg in range(4):
+                lanes = slice(lg * LANE, (lg + 1) * LANE)
+                for y in range(SIDE):
+                    v = tiles[t, y, core, :, lanes] * m + crecv[t, y, :, lanes] * om
+                    u = k * 8 + lg * 2
+                    s1[turned((y, z, x), core) + (slice(u, u + 2),)] = v.astype(jnp.bfloat16).reshape(2, SUB, LANE)
+
+    def send_group(g):
         z = lax.rem(where[1] + 1 + g, SIDE)
-
-        def compute(x, carry):
-            t = z * SIDE + x
-            left = steer[plan_ref[0, t]]
-            right = stacked[plan_ref[1, t]]
-            part = jnp.dot(left, right, preferred_element_type=jnp.float32)
-            tiles[t] = part.reshape(tiles.shape[1:])
-            core_copy(t).start()
-            return carry
-
-        lax.fori_loop(0, SIDE, compute, 0)
-        if g == 0:
-            mcopy.wait()
-
-        def combine(x, carry):
-            t = z * SIDE + x
-            core_copy(t).wait_recv()
-            for k in range(2):
-                m = mask[pl.ds(t * 2 + k, 1), :]
-                om = omask[pl.ds(t * 2 + k, 1), :]
-                for lg in range(4):
-                    lanes = slice(lg * LANE, (lg + 1) * LANE)
-                    for y in range(SIDE):
-                        v = tiles[t, y, core, :, lanes] * m + crecv[t, y, :, lanes] * om
-                        u = k * 8 + lg * 2
-                        s1[turned((y, z, x), core) + (slice(u, u + 2),)] = v.astype(jnp.bfloat16).reshape(2, SUB, LANE)
-            return carry
-
-        lax.fori_loop(0, SIDE, combine, 0)
         for d in NEAR_FIRST:
             send1(0, d, {1: z}, (0, g, d))
             send1(2, d, {1: z}, (2, g, d))
         if g < SIDE - 1:
             send1(1, g + 1, {}, (1, g + 1))
 
-    def all_core(t, carry):
-        core_copy(t).wait_send()
+    def both(i, carry):
+        compute(i)
+        combine(i - LAG)
         return carry
+
+    def first(i, carry):
+        compute(i)
+        return carry
+
+    def final(i, carry):
+        combine(i)
+        return carry
+
+    total = SIDE * SIDE
+    lax.fori_loop(0, LAG, first, 0)
+    mcopy.wait()
+    lax.fori_loop(LAG, SIDE + LAG, both, 0)
+    send_group(0)
+    lax.fori_loop(SIDE + LAG, 2 * SIDE + LAG, both, 0)
+    send_group(1)
+    lax.fori_loop(2 * SIDE + LAG, 3 * SIDE + LAG, both, 0)
+    send_group(2)
+    lax.fori_loop(3 * SIDE + LAG, total, both, 0)
+    lax.fori_loop(total - LAG, total, final, 0)
+    send_group(3)
 
     for g in range(2):
         row_done(0, g)
@@ -380,16 +406,16 @@
                 scene_ref[k, rows, lg * LANE : (lg + 1) * LANE] = re
                 scene_ref[k, rows, (lg + 2) * LANE : (lg + 3) * LANE] = im
 
-    gathers, forwards = {}, []
-
-    def gather(p, fixed, axis, d, key):
-        lo, hi, _ = PARTS[p]
+    gathers = {}
+
+    def gather(p, fixed, axis, d, key, step):
+        lo, hi, _ = GATHER_PARTS[p]
         src = wf.at[(core,) + pick(fixed, lo, hi)]
         n = len(gathers)
         cp = pltpu.make_async_remote_copy(
             src_ref=src,
             dst_ref=src,
-            send_sem=gsend.at[n],
+            send_sem=gsend.at[step],
             recv_sem=grecv.at[n],
             device_id=device_at(shifted(where, axis, d), core),
             device_id_type=MESH,
@@ -398,62 +424,63 @@
         gathers[key] = cp
 
     def forward(p, fixed):
-        lo, hi, _ = PARTS[p]
+        lo, hi, _ = GATHER_PARTS[p]
         src = wf.at[(core,) + pick(fixed, lo, hi)]
-        n = len(forwards)
         cp = pltpu.make_async_remote_copy(
             src_ref=src,
             dst_ref=src,
-            send_sem=fsend.at[n],
-            recv_sem=frecv.at[n],
+            send_sem=fsend.at[0],
+            recv_sem=frecv.at[0],
             device_id=other,
             device_id_type=MESH,
         )
         cp.start()
-        forwards.append(cp)
 
     def back(axis, d):
         return lax.rem(where[axis] + SIDE - d, SIDE)
 
-    order_of = (0, 2, 1)
+    order_of = (2, 0, 1)
     for p in order_of:
         for d in NEAR_FIRST:
-            gather(p, dict(enumerate(where)), PARTS[p][2][2], d, (p, "c", d))
+            gather(p, dict(enumerate(where)), GATHER_PARTS[p][2][2], d, (p, "c", d), 0)
 
     def row_out(p, r):
-        a, b, c = PARTS[p][2]
+        a, b, c = GATHER_PARTS[p][2]
         row = {a: where[a], b: back(b, r)}
-        for d in (1, 3):
-            gather(p, row, a, d, (p, r, d))
+        for d in NEAR_FIRST if r == LAST_ROW else (1, 3):
+            gather(p, row, a, d, (p, r, d), 2)
         forward(p, row)
 
     for p in order_of:
-        a, b, c = PARTS[p][2]
+        a, b, c = GATHER_PARTS[p][2]
         for d in NEAR_FIRST:
             gathers[p, "c", d].wait_recv()
         for d in NEAR_FIRST:
-            gather(p, {a: where[a], b: where[b]}, b, d, (p, "b", d))
+            gather(p, {a: where[a], b: where[b]}, b, d, (p, "b", d), 1)
         row_out(p, 0)
     for d in NEAR_FIRST:
         for p in order_of:
             gathers[p, "b", d].wait_recv()
             row_out(p, d)
-    rows_in = (0,) + NEAR_FIRST
-    for r in rows_in:
+    for r in (0, 1, 3):
         for p in order_of:
-            a, b, c = PARTS[p][2]
+            a, b, c = GATHER_PARTS[p][2]
             for d, half in ((1, slice(0, 2)), (3, slice(2, 4))):
                 gathers[p, r, d].wait_recv()
-                gather(p, {a: back(a, d), b: back(b, r), c: half}, a, d, (p, r, "far", d))
+                gather(p, {a: back(a, d), b: back(b, r), c: half}, a, d, (p, r, "far", d), 2)
                 forward(p, {a: back(a, d), b: back(b, r)})
-    for r in rows_in:
+    for r in (0, 1, 3):
         for p in order_of:
-            a, b, c = PARTS[p][2]
-            for d, half in ((1, slice(0, 2)), (3, slice(2, 4))):
+            a, b, c = GATHER_PARTS[p][2]
+            for d in (1, 3):
                 gathers[p, r, "far", d].wait_recv()
-                forward(p, {a: back(a, 2), b: back(b, r), c: half})
-    for cp in forwards:
-        cp.wait_recv()
+            forward(p, {a: back(a, 2), b: back(b, r)})
+    for d in NEAR_FIRST:
+        for p in order_of:
+            a, b, c = GATHER_PARTS[p][2]
+            gathers[p, LAST_ROW, d].wait_recv()
+            forward(p, {a: back(a, d), b: back(b, LAST_ROW)})
+    pltpu.make_async_copy(wf.at[1 - core], wf.at[1 - core], frecv.at[0]).wait()
 
     acc[...] = jnp.zeros_like(acc)
 
@@ -480,13 +507,22 @@
         acc[...] += jnp.sum(term.reshape(-1, 8, pulses), axis=0) * live
         return carry
 
-    lax.fori_loop(0, slots, backward, 0)
+    lax.fori_loop(0, slots, backward, 0, unroll=4)
     factor = -4.0 / math.sqrt(steer.shape[1] * (stacked.shape[2] // 2))
     grad_ref[...] = jnp.sum(acc[...], axis=0, keepdims=True) * factor
 
-    lax.fori_loop(0, 4 * SIDE, all_core, 0)
-    for cp in [*stage1.values(), *stage2.values(), *stage3.values(), *gathers.values(), *forwards]:
-        cp.wait_send()
+    def all_sent(like, sem):
+        pltpu.make_async_copy(like, like, sem).wait()
+
+    all_sent(crecv, csend.at[0])
+    all_sent(s1.at[:3], s1send.at[0])
+    all_sent(s1.at[0, :3], s2send.at[0])
+    for p in range(3):
+        all_sent(r3[p], s3send.at[p])
+    all_sent(wf.at[0, 0, 0, :3], gsend.at[0])
+    all_sent(wf.at[0, 0, :3], gsend.at[1])
+    all_sent(wf.at[0, :3], gsend.at[2])
+    all_sent(wf.at[core], fsend.at[0])
 
 
 def on_device(echoes, phases, kernel, steering, footprint, counts, range_start):
@@ -553,12 +589,12 @@
             vmem((8, pulses), f32),
             sem(slots + 3),
             sem(2),
-            sem(columns), sem(columns),
-            sem(27), sem(27),
-            sem(9), sem(9),
-            sem(9), sem(9),
-            sem(66), sem(66),
-            sem(60), sem(60),
+            sem(1), sem(columns),
+            sem(1), sem(27),
+            sem(1), sem(9),
+            sem(3), sem(9),
+            sem(3), sem(66),
+            sem(1), sem(1),
         ],
         compiler_params=pltpu.CompilerParams(
             collective_id=0, has_side_effects=True, vmem_limit_bytes=60 << 20

time: 89.7 us -> 85.6 us (0.954)
  Pallas kernels: 85.3 us -> 81.2 us
    pallas_call x1, Pallas kernels: 79.5 us -> 75.5 us  [on_device(): pl.pallas_call(main_kernel, out_shape=(jax.ShapeDtypeStruct((tile_rows, p...]
where the time goes in v3:
time: 85.6 us; the launch traced here: 85.4 us
  Pallas kernels  81.2 us (95%)
  local copies, waits for them, and re-layouts  2.82 us (3%)
  between operations  1.29 us (2%)
    pallas_call x1, Pallas kernels, on_device(): pl.pallas_call(main_kernel, out_shape=(jax.ShapeDtypeStruct((tile_rows, p...  75.5 us
    pallas_call x1, Pallas kernels, on_device(): pl.pallas_call(local_kernel, out_shape=(jax.ShapeDtypeStruct((6, columns)...  5.78 us
    unnamed x2, local copies, waits for them, and re-layouts  2.82 us

profile of v3, /device:TPU:1, one launch (start us, length us, event | category | flops | bytes accessed | tf_op | source)
XLA Modules:
  0.0 85.4 jit_solution(7693292979191226853)
XLA Ops:
  1.3 5.8 %shard_map.86 = (s32[6,16]{1,0:T(8,128)}, f32[32,128]{1,0:T(8,128)}, f32[2,512]{1,0:T(2,128)}, bf16[2,1024,512]{2,1,0:T(8,128)(2,1)}) custom-call(s32[1,12]{1,0:T(1,128)} %foot_ref.1, s32[1]{0:T(128)S(6)} %copy.12.count_ref, s32[1,2]{1,0:T(1,128)} %start_ref.1, f32[1,512]{1,0:T(1,128)} %bitcast.10, bf16[256,256]{1,0:T(8,128)(2,1)} %bitcast.8, ...), custom_call_target="tpu_custom_call" | custom-call | tf_op jit(solution)/shard_map/pallas_call | solution.py:547
  7.1 75.5 %shard_map.87 = (f32[2,32,512]{2,1,0:T(8,128)}, f32[1,512]{1,0:T(1,128)}) custom-call(s32[6,16]{1,0:T(8,128)} %get-tuple-element.8.plan_ref, f32[32,128]{1,0:T(8,128)} %get-tuple-element.9.mask_in, f32[2,512]{1,0:T(2,128)} %get-tuple-element.10.trig_in, bf16[2,1024,512]{2,1,0:T(8,128)(2,1)} %get-tuple-element.11.stacked_in, bf16[12,256,1024]{2,1,0:T(8,128)(2,1)} %bitcast.7), custom_call_target="tpu_custom_call" | custom-call | tf_op jit(solution)/shard_map/pallas_call | solution.py:563
  82.5 1.6 %copy.13 = f32[2,1,32,512]{3,2,1,0:T(8,128)} copy(f32[2,1,32,512]{3,2,1,0:T(8,128)} %bitcast.9) | data formatting | bytes 262144
  84.1 1.3 %copy.14 = f32[512]{0:T(512)} copy(f32[512]{0:T(512)} %bitcast.11) | data formatting | bytes 4096

commit v4 on v3

--- a/solution.py
+++ b/solution.py
@@ -65,6 +65,7 @@
     plan_ref,
     mask,
     trig,
+    stacked_out,
     stacked,
     windows,
     raw,
@@ -76,7 +77,7 @@
     last = (echoes_in.shape[2] - span) // LANE
     slots = foot_ref.shape[1]
     blocks = [jnp.minimum(start_ref[0, k] // LANE, last) for k in range(2)]
-    copies = []
+    copies, outs = [], []
     for k in range(2):
         cp = pltpu.make_async_copy(
             echoes_in.at[:, :, pl.ds(pl.multiple_of(blocks[k] * LANE, LANE), span)], windows.at[k], sem.at[k]
@@ -117,24 +118,26 @@
         weights = pltpu.roll(weights, start_ref[0, k] - blocks[k] * LANE, 0).astype(jnp.bfloat16)
         copies[k].wait()
 
-        def interpolate(i, carry):
-            at = pl.multiple_of(i * depth, depth)
+        for i in range(SIDE):
+            at = i * depth
             window = windows[k, pl.ds(at, depth)]
             value = jnp.dot(window.reshape(2 * depth, span), weights, preferred_element_type=jnp.float32)
             top, low = pl.ds(at, depth), pl.ds(pulses + at, depth)
             for h in range(breadth // LANE):
-                raw[h] = value[:, h * LANE : (h + 1) * LANE]
-                re = raw[h, pl.ds(0, depth, stride=2), :].astype(jnp.bfloat16)
-                im = raw[h, pl.ds(1, depth, stride=2), :].astype(jnp.bfloat16)
+                raw[i, h] = value[:, h * LANE : (h + 1) * LANE]
+                re = raw[i, h, pl.ds(0, depth, stride=2), :].astype(jnp.bfloat16)
+                im = raw[i, h, pl.ds(1, depth, stride=2), :].astype(jnp.bfloat16)
                 left = slice(h * LANE, (h + 1) * LANE)
                 right = slice(breadth + h * LANE, breadth + (h + 1) * LANE)
                 stacked[k, top, left] = re
                 stacked[k, top, right] = im
                 stacked[k, low, left] = -im
                 stacked[k, low, right] = re
-            return carry
-
-        lax.fori_loop(0, SIDE, interpolate, 0)
+        out = pltpu.make_async_copy(stacked.at[k], stacked_out.at[k], sem.at[2 + k])
+        out.start()
+        outs.append(out)
+    for out in outs:
+        out.wait()
 
 
 def main_kernel(
@@ -264,7 +267,7 @@
             s2[p][here] = v.astype(jnp.bfloat16)
             return carry
 
-        lax.fori_loop(0, SIDE, add, 0)
+        lax.fori_loop(0, SIDE, add, 0, unroll=True)
 
     def send2(p, d):
         b = PARTS[p][2][1]
@@ -357,16 +360,16 @@
         return carry
 
     total = SIDE * SIDE
-    lax.fori_loop(0, LAG, first, 0)
+    lax.fori_loop(0, LAG, first, 0, unroll=2)
     mcopy.wait()
-    lax.fori_loop(LAG, SIDE + LAG, both, 0)
+    lax.fori_loop(LAG, SIDE + LAG, both, 0, unroll=2)
     send_group(0)
-    lax.fori_loop(SIDE + LAG, 2 * SIDE + LAG, both, 0)
+    lax.fori_loop(SIDE + LAG, 2 * SIDE + LAG, both, 0, unroll=2)
     send_group(1)
-    lax.fori_loop(2 * SIDE + LAG, 3 * SIDE + LAG, both, 0)
+    lax.fori_loop(2 * SIDE + LAG, 3 * SIDE + LAG, both, 0, unroll=2)
     send_group(2)
-    lax.fori_loop(3 * SIDE + LAG, total, both, 0)
-    lax.fori_loop(total - LAG, total, final, 0)
+    lax.fori_loop(3 * SIDE + LAG, total, both, 0, unroll=2)
+    lax.fori_loop(total - LAG, total, final, 0, unroll=2)
     send_group(3)
 
     for g in range(2):
@@ -553,11 +556,12 @@
             jax.ShapeDtypeStruct((tile_rows, 2 * pulses, width), bf16),
         ),
         in_specs=[smem] * 3 + [whole] * 2 + [anywhere],
-        out_specs=[smem] + [whole] * 3,
+        out_specs=[smem] + [whole] * 2 + [anywhere],
         scratch_shapes=[
+            vmem((tile_rows, 2 * pulses, width), bf16),
             vmem((tile_rows, pulses, 2, span), bf16),
-            vmem((breadth // LANE, 2 * pulses // SIDE, LANE), f32),
-            sem(2),
+            vmem((SIDE, breadth // LANE, 2 * pulses // SIDE, LANE), f32),
+            sem(4),
         ],
     )(footprint, counts, range_start, phases[None], kernel[0], echoes)
     scene, grad = pl.pallas_call(

time: 85.6 us -> 84.8 us (level)
  no operation moved by 1% of the time
where the time goes in v4:
time: 84.8 us; the launch traced here: 84.5 us
  Pallas kernels  80.4 us (95%)
  local copies, waits for them, and re-layouts  2.82 us (3%)
  between operations  1.29 us (2%)
    pallas_call x1, Pallas kernels, on_device(): pl.pallas_call(main_kernel, out_shape=(jax.ShapeDtypeStruct((tile_rows, p...  75.4 us
    pallas_call x1, Pallas kernels, on_device(): pl.pallas_call(local_kernel, out_shape=(jax.ShapeDtypeStruct((6, columns)...  5.01 us
    unnamed x2, local copies, waits for them, and re-layouts  2.82 us

profile of v4, /device:TPU:1, one launch (start us, length us, event | category | flops | bytes accessed | tf_op | source)
XLA Modules:
  0.0 84.5 jit_solution(2862232170228575509)
XLA Ops:
  1.3 5.0 %shard_map.86 = (s32[6,16]{1,0:T(8,128)}, f32[32,128]{1,0:T(8,128)}, f32[2,512]{1,0:T(2,128)}, bf16[2,1024,512]{2,1,0:T(8,128)(2,1)}) custom-call(s32[1,12]{1,0:T(1,128)} %foot_ref.1, s32[1]{0:T(128)S(6)} %copy.12.count_ref, s32[1,2]{1,0:T(1,128)} %start_ref.1, f32[1,512]{1,0:T(1,128)} %bitcast.10, bf16[256,256]{1,0:T(8,128)(2,1)} %bitcast.8, ...), custom_call_target="tpu_custom_call" | custom-call | tf_op jit(solution)/shard_map/pallas_call | solution.py:550
  6.3 75.4 %shard_map.87 = (f32[2,32,512]{2,1,0:T(8,128)}, f32[1,512]{1,0:T(1,128)}) custom-call(s32[6,16]{1,0:T(8,128)} %get-tuple-element.8.plan_ref, f32[32,128]{1,0:T(8,128)} %get-tuple-element.9.mask_in, f32[2,512]{1,0:T(2,128)} %get-tuple-element.10.trig_in, bf16[2,1024,512]{2,1,0:T(8,128)(2,1)} %get-tuple-element.11.stacked_in, bf16[12,256,1024]{2,1,0:T(8,128)(2,1)} %bitcast.7), custom_call_target="tpu_custom_call" | custom-call | tf_op jit(solution)/shard_map/pallas_call | solution.py:567
  81.7 1.6 %copy.13 = f32[2,1,32,512]{3,2,1,0:T(8,128)} copy(f32[2,1,32,512]{3,2,1,0:T(8,128)} %bitcast.9) | data formatting | bytes 262144
  83.3 1.3 %copy.14 = f32[512]{0:T(512)} copy(f32[512]{0:T(512)} %bitcast.11) | data formatting | bytes 4096

commit v5 on v4

--- a/solution.py
+++ b/solution.py
@@ -140,14 +140,20 @@
         out.wait()
 
 
+def hand_on(scene_in, grad_in, scene_out, grad_out):
+    scene_out[...] = scene_in[...]
+    grad_out[...] = jnp.sum(grad_in[...], axis=0, keepdims=True)
+
+
 def main_kernel(
     plan_ref,
     mask_in,
     trig_in,
     stacked_in,
     steer_in,
+    scene_out,
+    grad_ref,
     scene_ref,
-    grad_ref,
     mask,
     omask,
     trig,
@@ -409,6 +415,9 @@
                 scene_ref[k, rows, lg * LANE : (lg + 1) * LANE] = re
                 scene_ref[k, rows, (lg + 2) * LANE : (lg + 3) * LANE] = im
 
+    scene_copy = pltpu.make_async_copy(scene_ref, scene_out, lsem.at[0])
+    scene_copy.start()
+
     gathers = {}
 
     def gather(p, fixed, axis, d, key, step):
@@ -512,8 +521,9 @@
 
     lax.fori_loop(0, slots, backward, 0, unroll=4)
     factor = -4.0 / math.sqrt(steer.shape[1] * (stacked.shape[2] // 2))
-    grad_ref[...] = jnp.sum(acc[...], axis=0, keepdims=True) * factor
-
+    grad_ref[...] = acc[...] * factor
+
+    scene_copy.wait()
     def all_sent(like, sem):
         pltpu.make_async_copy(like, like, sem).wait()
 
@@ -568,11 +578,12 @@
         main_kernel,
         out_shape=(
             jax.ShapeDtypeStruct((tile_rows, part_rows, width), f32),
-            jax.ShapeDtypeStruct((1, pulses), f32),
+            jax.ShapeDtypeStruct((8, pulses), f32),
         ),
         in_specs=[smem] + [anywhere] * 4,
-        out_specs=[whole] * 2,
+        out_specs=[anywhere, whole],
         scratch_shapes=[
+            vmem((tile_rows, part_rows, width), f32),
             vmem((columns * tile_rows, LANE), f32),
             vmem((columns * tile_rows, LANE), f32),
             vmem((2, pulses), f32),
@@ -604,6 +615,15 @@
             collective_id=0, has_side_effects=True, vmem_limit_bytes=60 << 20
         ),
     )(plan, mask, trig, stacked, steering[0])
+    scene, grad = pl.pallas_call(
+        hand_on,
+        out_shape=(
+            jax.ShapeDtypeStruct(scene.shape, f32),
+            jax.ShapeDtypeStruct((1, pulses), f32),
+        ),
+        in_specs=[whole] * 2,
+        out_specs=[whole] * 2,
+    )(scene, grad)
     return (scene[:, None], grad[0])
 
 

time: 84.8 us -> 83.3 us (0.982)
  local copies, waits for them, and re-layouts: 2.82 us -> 0 us
  Pallas kernels: 80.4 us -> 81.8 us
    unnamed x2 -> x0, local copies, waits for them, and re-layouts: 2.82 us -> none
    pallas_call x0 -> x1, Pallas kernels: none -> 1.57 us  [on_device(): pl.pallas_call(hand_on, out_shape=(jax.ShapeDtypeStruct(scene.shape, f32)...]
where the time goes in v5:
time: 83.3 us; the launch traced here: 83.1 us
  Pallas kernels  81.8 us (98%)
  between operations  1.29 us (2%)
    pallas_call x1, Pallas kernels, on_device(): pl.pallas_call(main_kernel, out_shape=(jax.ShapeDtypeStruct((tile_rows, p...  75.3 us
    pallas_call x1, Pallas kernels, on_device(): pl.pallas_call(local_kernel, out_shape=(jax.ShapeDtypeStruct((6, columns)...  5 us

profile of v5, /device:TPU:1, one launch (start us, length us, event | category | flops | bytes accessed | tf_op | source)
XLA Modules:
  0.0 83.1 jit_solution(8704024508639770133)
XLA Ops:
  1.3 5.0 %shard_map.86 = (s32[6,16]{1,0:T(8,128)}, f32[32,128]{1,0:T(8,128)}, f32[2,512]{1,0:T(2,128)}, bf16[2,1024,512]{2,1,0:T(8,128)(2,1)}) custom-call(s32[1,12]{1,0:T(1,128)} %foot_ref.1, s32[1]{0:T(128)S(6)} %copy.10.count_ref, s32[1,2]{1,0:T(1,128)} %start_ref.1, f32[1,512]{1,0:T(1,128)} %bitcast.9, bf16[256,256]{1,0:T(8,128)(2,1)} %bitcast.8, ...), custom_call_target="tpu_custom_call" | custom-call | tf_op jit(solution)/shard_map/pallas_call | solution.py:560
  6.3 75.3 %shard_map.87 = (f32[2,32,512]{2,1,0:T(8,128)}, f32[8,512]{1,0:T(8,128)}) custom-call(s32[6,16]{1,0:T(8,128)} %get-tuple-element.10.plan_ref, f32[32,128]{1,0:T(8,128)} %get-tuple-element.11.mask_in, f32[2,512]{1,0:T(2,128)} %get-tuple-element.12.trig_in, bf16[2,1024,512]{2,1,0:T(8,128)(2,1)} %get-tuple-element.13.stacked_in, bf16[12,256,1024]{2,1,0:T(8,128)(2,1)} %bitcast.7), custom_call_target="tpu_custom_call" | custom-call | tf_op jit(solution)/shard_map/pallas_call | solution.py:577
  81.6 1.6 %shard_map.88 = (f32[2,32,512]{2,1,0:T(8,128)}, f32[1,512]{1,0:T(1,128)}) custom-call(f32[2,32,512]{2,1,0:T(8,128)} %get-tuple-element.14.scene_in, f32[8,512]{1,0:T(8,128)} %get-tuple-element.15.grad_in), custom_call_target="tpu_custom_call" | custom-call | tf_op jit(solution)/shard_map/pallas_call | solution.py:618

commit v6 on v5

--- a/solution.py
+++ b/solution.py
@@ -470,17 +470,25 @@
         for d in NEAR_FIRST:
             gather(p, {a: where[a], b: where[b]}, b, d, (p, "b", d), 1)
         row_out(p, 0)
-    for d in NEAR_FIRST:
+    def rows_on(d):
         for p in order_of:
             gathers[p, "b", d].wait_recv()
             row_out(p, d)
-    for r in (0, 1, 3):
+
+    def near_in(r):
         for p in order_of:
             a, b, c = GATHER_PARTS[p][2]
             for d, half in ((1, slice(0, 2)), (3, slice(2, 4))):
                 gathers[p, r, d].wait_recv()
                 gather(p, {a: back(a, d), b: back(b, r), c: half}, a, d, (p, r, "far", d), 2)
                 forward(p, {a: back(a, d), b: back(b, r)})
+
+    rows_on(1)
+    rows_on(3)
+    near_in(0)
+    rows_on(2)
+    near_in(1)
+    near_in(3)
     for r in (0, 1, 3):
         for p in order_of:
             a, b, c = GATHER_PARTS[p][2]

time: 83.3 us -> 83 us (level)
  no operation moved by 1% of the time
where the time goes in v6:
time: 83 us; the launch traced here: 82.8 us
  Pallas kernels  81.5 us (98%)
  between operations  1.29 us (2%)
    pallas_call x1, Pallas kernels, on_device(): pl.pallas_call(main_kernel, out_shape=(jax.ShapeDtypeStruct((tile_rows, p...  74.9 us
    pallas_call x1, Pallas kernels, on_device(): pl.pallas_call(local_kernel, out_shape=(jax.ShapeDtypeStruct((6, columns)...  5 us

profile of v6, /device:TPU:1, one launch (start us, length us, event | category | flops | bytes accessed | tf_op | source)
XLA Modules:
  0.0 82.8 jit_solution(292378282085184049)
XLA Ops:
  1.3 5.0 %shard_map.86 = (s32[6,16]{1,0:T(8,128)}, f32[32,128]{1,0:T(8,128)}, f32[2,512]{1,0:T(2,128)}, bf16[2,1024,512]{2,1,0:T(8,128)(2,1)}) custom-call(s32[1,12]{1,0:T(1,128)} %foot_ref.1, s32[1]{0:T(128)S(6)} %copy.10.count_ref, s32[1,2]{1,0:T(1,128)} %start_ref.1, f32[1,512]{1,0:T(1,128)} %bitcast.9, bf16[256,256]{1,0:T(8,128)(2,1)} %bitcast.8, ...), custom_call_target="tpu_custom_call" | custom-call | tf_op jit(solution)/shard_map/pallas_call | solution.py:568
  6.3 74.9 %shard_map.87 = (f32[2,32,512]{2,1,0:T(8,128)}, f32[8,512]{1,0:T(8,128)}) custom-call(s32[6,16]{1,0:T(8,128)} %get-tuple-element.10.plan_ref, f32[32,128]{1,0:T(8,128)} %get-tuple-element.11.mask_in, f32[2,512]{1,0:T(2,128)} %get-tuple-element.12.trig_in, bf16[2,1024,512]{2,1,0:T(8,128)(2,1)} %get-tuple-element.13.stacked_in, bf16[12,256,1024]{2,1,0:T(8,128)(2,1)} %bitcast.7), custom_call_target="tpu_custom_call" | custom-call | tf_op jit(solution)/shard_map/pallas_call | solution.py:585
  81.2 1.6 %shard_map.88 = (f32[2,32,512]{2,1,0:T(8,128)}, f32[1,512]{1,0:T(1,128)}) custom-call(f32[2,32,512]{2,1,0:T(8,128)} %get-tuple-element.14.scene_in, f32[8,512]{1,0:T(8,128)} %get-tuple-element.15.grad_in), custom_call_target="tpu_custom_call" | custom-call | tf_op jit(solution)/shard_map/pallas_call | solution.py:626
